TPU v7x, 32 devices: a whole 2x2x4 slice. The times are simulated.
32 devices in a mesh: grp: 2 (over y), row: 4 (over z), col: 4 (over x, core).
Axes of the slice: x: 2, y: 2, z: 4, core: 2. Of those that a mesh axis runs over, the one named last changes fastest.
Arguments:
- activations: bfloat16 [1024, 6144], P(('grp', 'col'), 'row'), parts along dimension 0, may hold values from -6 to 6
- out_grads: bfloat16 [1024, 18432], P(('grp', 'row'), 'col'), parts along dimension 0, may hold values from -0.1796875 to 0.1796875
- matrix: bfloat16 [12288, 18432], P(('grp', 'row'), 'col'), parts along dimension 0, may hold values from -30 to 30
- left: bfloat16 [12288, 256], P(('grp', 'row')), parts along dimension 0, may hold values from -4 to 4
- right: bfloat16 [36864, 256], P(('grp', 'col')), parts along dimension 0, may hold values from -4 to 4
Outputs:
- left_new: bfloat16 [12288, 256], P(('grp', 'row')), parts along dimension 0
- right_new: bfloat16 [36864, 256], P(('grp', 'col')), parts along dimension 0
- residual: bfloat16 [12288, 18432], P(('grp', 'row'), 'col'), parts along dimension 0
There are 2 independent parts, one for each index of `grp`. A program takes and returns all parts, laid end to end along the dimension named above; each array names one. Nothing has to cross between parts.
All inputs are finite; a program needn't handle non-finite values.
Results may differ from a plain program's by a relative error of at most 0.0034.
Values may be sent and summed in bfloat16 or wider, within the bound.
No kernel may reach another device: no remote copies, remote signals or barrier semaphores. Data moves between devices by JAX's collectives and lax.ppermute only.
A program may use at most 192 MiB of HBM per device.

v0:
```python
import functools
import math
import jax
import jax.numpy as jnp
from jax import lax
from jax.experimental import pallas as pl
from jax.experimental.pallas import tpu as pltpu
from jax.sharding import PartitionSpec as P

f32 = jnp.float32
bf16 = jnp.bfloat16
NT = (((1,), (1,)), ((), ()))
epsilon = 1e-06
BLOCK = 768
WIDE = 384
TILE = 768
MB = 1 << 20
LIMIT = 48 * MB


def near(x):
    return pltpu.with_memory_space_constraint(x, pltpu.VMEM)


def far(x):
    return pltpu.with_memory_space_constraint(x, pltpu.HBM)


def pick(extent, want, offset=0):
    for size in range(min(want, extent), 0, -1):
        if extent % size == 0 and offset % size == 0 and (size % 128 == 0 or size == extent):
            return size
    return extent


def each(count, unroll, step):
    if unroll:
        for i in range(count):
            step(i)
    else:
        pl.loop(0, count)(step)


def span(i, tile):
    return pl.ds(i * tile, tile) if isinstance(i, int) else pl.ds(pl.multiple_of(i * tile, tile), tile)


UNROLL = True


def fold(x):
    rows, cols = x.shape
    y = x.reshape(rows // 8, 8, cols).sum(axis=0)
    out = y[:, :128]
    for at in range(128, cols, 128):
        out = out + y[:, at:at + 128]
    return out


def first_kernel(groups, tile, has_prev, *refs):
    at_ref, w_ref, l_ref, r_ref = refs[:4]
    used = 4
    parts = []
    for count in groups:
        parts.append(refs[used:used + count])
        used += count
    if has_prev:
        acc_in = refs[used]
        used += 2
    f_ref, acc_ref, g_ref = refs[used:used + 3]
    step = pl.program_id(0)
    at = 0
    for part in parts:
        total = part[0][...]
        for more in part[1:]:
            total = total + more[...]
        g_ref[pl.ds(at, total.shape[0]), :] = total
        at += total.shape[0]

    @pl.when(step == 0)
    def _():
        if has_prev:
            acc_ref[...] = acc_in[...]
        else:
            acc_ref[...] = jnp.zeros_like(acc_ref)

    m = at_ref.shape[0]

    def step_rows(i):
        rows = span(i, tile)
        grad = jnp.dot(at_ref[rows, :], g_ref[...], preferred_element_type=f32)
        image = lax.dot_general(l_ref[rows, :], r_ref[...], NT, preferred_element_type=f32)
        w = w_ref[rows, :].astype(f32)
        x = w * grad
        fisher = 1.0 + x * x
        f_ref[rows, :] = fisher.astype(f_ref.dtype)
        weighted = (fisher * (w - image)).astype(bf16)
        acc_ref[rows, :] += jnp.dot(weighted, r_ref[...], preferred_element_type=f32)
    each(m // tile, UNROLL, step_rows)


def first_pass(at, w, left, right, groups, offset, width, prev, block=512, tile=512, fdt=bf16):
    m, n = w.shape
    rank = left.shape[1]
    tokens = at.shape[1]
    bn = pick(width, block, offset)
    tile = pick(m, tile)
    base = offset // bn
    flat = [p for g in groups for p in g]
    ins = [near(at), far(w), far(left), far(right)] + [far(p[0]) for p in flat]

    def piece(array, rows, row, whole):
        shift = base if whole else 0
        return pl.BlockSpec((rows, bn), lambda j: (row, shift + j))

    specs = [
        pl.BlockSpec((m, tokens), lambda j: (0, 0)),
        pl.BlockSpec((m, bn), lambda j: (0, base + j)),
        pl.BlockSpec((m, rank), lambda j: (0, 0)),
        pl.BlockSpec((bn, rank), lambda j: (base + j, 0)),
    ] + [piece(*p) for p in flat]
    alias = {}
    if prev is not None:
        fprev, accprev = prev
        alias = {len(ins): 1, len(ins) + 1: 0}
        ins += [near(accprev), far(fprev)]
        specs += [pl.BlockSpec((m, rank), lambda j: (0, 0)), pl.BlockSpec(memory_space=pl.ANY)]
    cost = pl.CostEstimate(flops=2 * m * width * (tokens + 2 * rank), bytes_accessed=m * width * 4, transcendentals=0)
    return pl.pallas_call(
        functools.partial(first_kernel, tuple(len(g) for g in groups), tile, prev is not None),
        grid=(width // bn,),
        in_specs=specs,
        out_specs=[pl.BlockSpec((m, bn), lambda j: (0, base + j)), pl.BlockSpec((m, rank), lambda j: (0, 0))],
        out_shape=[pltpu.HBM((m, n), fdt), pltpu.VMEM((m, rank), f32)],
        scratch_shapes=[pltpu.VMEM((tokens, bn), bf16)],
        input_output_aliases=alias,
        compiler_params=pltpu.CompilerParams(vmem_limit_bytes=LIMIT),
        cost_estimate=cost,
        name="first_pass",
    )(*ins)


def total_of(refs):
    if len(refs) == 4:
        return (refs[0][...] + refs[2][...]) + (refs[1][...] + refs[3][...])
    return refs[0][...]


def step_of(total, copies):
    curve = jnp.sum(total[0], axis=(0, 1), keepdims=True)
    norm = jnp.sum(total[1], axis=(0, 1), keepdims=True) * (1.0 / copies)
    return norm / (curve + epsilon)


def left_curve_kernel(tile, side_ref, b_ref, c_ref, r_ref, f_ref, o_ref, d_ref, a_ref):
    m = d_ref.shape[0]
    half = m // 2

    @pl.when(pl.program_id(0) == 0)
    def _():
        low = side_ref[0, 0] == 0
        total = jnp.zeros((8, 128), f32)
        for at, first, second in ((0, b_ref, c_ref), (half, c_ref, b_ref)):
            d = jnp.where(low, first[...], second[...])
            d_ref[pl.ds(at, half), :] = d
            a_ref[pl.ds(at, half), :] = d.astype(bf16)
            total = total + fold(d * d)
        o_ref[0] = jnp.zeros((8, 128), f32)
        o_ref[1] = total

    def step_rows(i):
        rows = span(i, tile)
        image = lax.dot_general(a_ref[rows, :], r_ref[...], NT, preferred_element_type=f32)
        o_ref[0] += fold(f_ref[rows, :].astype(f32) * (image * image))
    each(m // tile, UNROLL, step_rows)


def left_curve(side, halves, right, f):
    m, n = f.shape
    rank = right.shape[1]
    bn = pick(n, 2 * BLOCK)
    half = pl.BlockSpec((m // 2, rank), lambda j: (0, 0))
    return pl.pallas_call(
        functools.partial(left_curve_kernel, pick(m, TILE)),
        grid=(n // bn,),
        in_specs=[pl.BlockSpec(memory_space=pltpu.SMEM), half, half, pl.BlockSpec((bn, rank), lambda j: (j, 0)),
                  pl.BlockSpec((m, bn), lambda j: (0, j))],
        out_specs=[pl.BlockSpec((2, 8, 128), lambda j: (0, 0, 0)), pl.BlockSpec((m, rank), lambda j: (0, 0))],
        out_shape=[jax.ShapeDtypeStruct((2, 8, 128), f32), pltpu.VMEM((m, rank), f32)],
        scratch_shapes=[pltpu.VMEM((m, rank), bf16)],
        compiler_params=pltpu.CompilerParams(vmem_limit_bytes=LIMIT),
        cost_estimate=pl.CostEstimate(flops=2 * m * n * rank, bytes_accessed=2 * m * n, transcendentals=0),
        name="left_curve",
    )(side, *halves, far(right), far(f))


def right_curve_kernel(tile, flag_ref, a_ref, t_ref, b_ref, f_ref, i_ref, o_ref, q_ref):
    m = a_ref.shape[0]
    own = flag_ref[0, 0] > 0
    q = jnp.where(own, t_ref[...].astype(f32), b_ref[...].astype(f32))
    q_ref[...] = q.astype(bf16)

    @pl.when(pl.program_id(0) == 0)
    def _():
        o_ref[...] = i_ref[...]

    o_ref[1] += fold(q * q)

    def step_rows(i):
        rows = span(i, tile)
        image = jnp.dot(a_ref[rows, :], q_ref[...], preferred_element_type=f32)
        o_ref[0] += fold(f_ref[rows, :].astype(f32) * (image * image))
    each(m // tile, UNROLL, step_rows)


def right_curve(flag, left_new, total, back, f, sums, offset, width):
    m, rank = left_new.shape
    bn = pick(width, 2 * BLOCK, offset)
    base = offset // bn
    tall = pl.BlockSpec((rank, bn), lambda j: (0, j))
    small = pl.BlockSpec((2, 8, 128), lambda j: (0, 0, 0))
    return pl.pallas_call(
        functools.partial(right_curve_kernel, pick(m, TILE)),
        grid=(width // bn,),
        in_specs=[pl.BlockSpec(memory_space=pltpu.SMEM), pl.BlockSpec((m, rank), lambda j: (0, 0)), tall, tall,
                  pl.BlockSpec((m, bn), lambda j: (0, base + j)), small],
        out_specs=[small, tall],
        out_shape=[jax.ShapeDtypeStruct((2, 8, 128), f32), jax.ShapeDtypeStruct((rank, width), bf16)],
        compiler_params=pltpu.CompilerParams(vmem_limit_bytes=LIMIT),
        cost_estimate=pl.CostEstimate(flops=2 * m * width * rank, bytes_accessed=2 * m * width, transcendentals=0),
        name="right_curve",
    )(flag, far(left_new), total, back, far(f), sums)


def left_new_kernel(copies, *refs):
    l_ref, d_ref = refs[:2]
    step_ref, new_ref, t_ref, pair_ref = refs[-4:]
    rank = l_ref.shape[1]
    step = step_of(total_of(refs[2:-4]), copies)
    step_ref[...] = jnp.broadcast_to(step, (8, 128))
    left = l_ref[...].astype(f32)
    descent = d_ref[...]
    new = left + step * descent
    new_ref[...] = new.astype(bf16)
    t_ref[...] = new.T.astype(bf16)
    moved = left + step * descent.astype(bf16).astype(f32)
    high = moved.astype(bf16)
    pair_ref[:, :rank] = high
    pair_ref[:, rank:] = (moved - high.astype(f32)).astype(bf16)


def left_update(left, descent, pieces, copies):
    m, rank = left.shape
    return pl.pallas_call(
        functools.partial(left_new_kernel, copies),
        out_shape=[jax.ShapeDtypeStruct((8, 128), f32), pltpu.HBM((m, rank), bf16), pltpu.VMEM((rank, m), bf16),
                   pltpu.VMEM((m, 2 * rank), bf16)],
        compiler_params=pltpu.CompilerParams(vmem_limit_bytes=LIMIT),
        cost_estimate=pl.CostEstimate(flops=2 * m * rank, bytes_accessed=10 * m * rank, transcendentals=0),
        name="left_update",
    )(far(left), near(descent), *pieces)


def partial_kernel(tile, p_ref, w_ref, r_ref, f_ref, t_ref, k_ref, o_ref, acc_ref):
    m = p_ref.shape[0]
    acc_ref[...] = jnp.zeros_like(acc_ref)

    def step_rows(i):
        rows = span(i, tile)
        image = lax.dot_general(p_ref[rows, :], r_ref[...], NT, preferred_element_type=f32)
        later = w_ref[rows, :].astype(f32) - image
        weighted = (f_ref[rows, :].astype(f32) * later).astype(bf16)
        acc_ref[...] += jnp.dot(t_ref[:, rows], weighted, preferred_element_type=f32)
    each(m // tile, UNROLL, step_rows)
    o_ref[...] = acc_ref[...].astype(o_ref.dtype)


def partial_pass(pair, w, twice, f, new_t, token, offset, width):
    m, n = w.shape
    rank = new_t.shape[0]
    bn = pick(width, WIDE, offset)
    base = offset // bn
    tile = pick(m, TILE)
    wide = pl.BlockSpec((m, bn), lambda j: (0, base + j))
    return pl.pallas_call(
        functools.partial(partial_kernel, tile),
        grid=(width // bn,),
        in_specs=[pl.BlockSpec((m, 2 * rank), lambda j: (0, 0)), wide,
                  pl.BlockSpec((bn, 2 * rank), lambda j: (base + j, 0)), wide,
                  pl.BlockSpec((rank, m), lambda j: (0, 0)), pl.BlockSpec(memory_space=pl.ANY)],
        out_specs=pl.BlockSpec((rank, bn), lambda j: (0, j)),
        out_shape=jax.ShapeDtypeStruct((rank, width), bf16),
        scratch_shapes=[pltpu.VMEM((rank, bn), f32)],
        compiler_params=pltpu.CompilerParams(vmem_limit_bytes=LIMIT),
        cost_estimate=pl.CostEstimate(flops=6 * m * width * rank, bytes_accessed=4 * m * width, transcendentals=0),
        name="partial_pass",
    )(near(pair), far(w), far(twice), far(f), near(new_t), token)


def last_kernel(tile, copies, edges, *refs):
    w_ref, p_ref, r_ref, n_ref = refs[:4]
    q_refs = refs[4:4 + len(edges)]
    pieces = refs[4 + len(edges):-3]
    o_ref, new_ref, q_ref = refs[-3:]
    j = pl.program_id(0)
    s2 = step_of(total_of(pieces), copies)
    m = p_ref.shape[0]
    rank = n_ref.shape[1]
    for (first, count), ref in zip(edges, q_refs):
        @pl.when((j >= first) & (j < first + count))
        def _():
            q_ref[...] = ref[...]

    def step_rows(i):
        rows = span(i, tile)
        image = lax.dot_general(p_ref[rows, :], r_ref[...], NT, preferred_element_type=f32)
        second = jnp.dot(n_ref[rows, :], q_ref[...], preferred_element_type=f32)
        later = w_ref[rows, :].astype(f32) - image
        o_ref[rows, :] = (later - s2 * second).astype(o_ref.dtype)
    each(m // tile, UNROLL, step_rows)
    new_ref[...] = (r_ref[:, :rank].astype(f32) + s2 * q_ref[...].astype(f32).T).astype(bf16)


def last_pass(w, pair, twice, left_new, parts, pieces, copies):
    m, n = w.shape
    rank = left_new.shape[1]
    common = n
    at = 0
    edges = []
    for part in parts:
        common = math.gcd(common, part.shape[1])
    bn = pick(common, 3 * BLOCK // 2)
    for part in parts:
        edges.append((at // bn, part.shape[1] // bn))
        at += part.shape[1]
    whole = pl.BlockSpec((m, rank), lambda j: (0, 0))
    wide = pl.BlockSpec((m, bn), lambda j: (0, j))
    side = pl.BlockSpec((bn, rank), lambda j: (j, 0))

    def tall(first, count):
        return pl.BlockSpec((rank, bn), lambda j: (0, jnp.clip(j - first, 0, count - 1)))

    return pl.pallas_call(
        functools.partial(last_kernel, pick(m, TILE), copies, tuple(edges)),
        grid=(n // bn,),
        in_specs=[wide, pl.BlockSpec((m, 2 * rank), lambda j: (0, 0)), pl.BlockSpec((bn, 2 * rank), lambda j: (j, 0)), whole]
        + [tall(*edge) for edge in edges]
        + [pl.BlockSpec((2, 8, 128), lambda j: (0, 0, 0))] * len(pieces),
        out_specs=[wide, side],
        out_shape=[jax.ShapeDtypeStruct((m, n), bf16), jax.ShapeDtypeStruct((n, rank), bf16)],
        scratch_shapes=[pltpu.VMEM((rank, bn), bf16)],
        compiler_params=pltpu.CompilerParams(vmem_limit_bytes=LIMIT),
        cost_estimate=pl.CostEstimate(flops=6 * m * n * rank, bytes_accessed=4 * m * n, transcendentals=0),
        name="last_pass",
    )(far(w), near(pair), far(twice), far(left_new), *parts, *pieces)


FIRST = (3, 2, 1)
SECOND = (1, 1, 1, 1)
ORDER = (
    ("p", 0), ("p", 1), ("p", 2), ("h", 0), ("p", 3), ("h", 1), ("t", 0), ("h", 2), ("t", 1),
    ("h", 3), ("v", 0), ("t", 2), ("v", 1), ("t", 3), ("v", 2), ("v", 3),
)


def cut(extent, weights):
    units = extent // 128 if extent % 128 == 0 else 1
    size = extent // units
    total = sum(weights)
    edges = [0]
    seen = 0
    for weight in weights:
        seen += weight
        edges.append(units * seen // total)
    return [(a * size, (b - a) * size) for a, b in zip(edges, edges[1:]) if b > a]


def other(count, bit):
    return [(i, i ^ bit) for i in range(count)]


def turned(count, by):
    return [(i, (i + by) % count) for i in range(count)]


def pieces_of(x, axis):
    if lax.axis_size(axis) == 4:
        return [x] + [lax.ppermute(x, axis, turned(4, k)) for k in (1, 2, 3)]
    return [add_up(x, axis)]


def add_up(x, axis):
    count = lax.axis_size(axis)
    if count == 4:
        own, one, two, three = pieces_of(x, axis)
        return (own + two) + (one + three)
    if count & (count - 1):
        return lax.psum(x, axis)
    bit = 1
    while bit < count:
        x = x + lax.ppermute(x, axis, other(count, bit))
        bit *= 2
    return x


def line_order(axis):
    at = lax.axis_index(axis)
    low = at < 2
    return [at, at ^ 1, jnp.where(low, 2, 1), jnp.where(low, 3, 0)]


def sum_columns(x, axis):
    count = lax.axis_size(axis)
    if count != 4 or x.shape[0] % 32:
        whole = lax.psum(x, axis)
        return whole[:x.shape[0] // 2], whole[x.shape[0] // 2:]
    side = lax.axis_index(axis) & 1
    half = x.shape[0] // 2
    mine = lax.dynamic_slice_in_dim(x, side * half, half, 0)
    theirs = lax.dynamic_slice_in_dim(x, (1 - side) * half, half, 0)
    chip = (mine + lax.ppermute(theirs, axis, other(4, 1))).astype(bf16)
    both = chip.astype(f32) + lax.ppermute(chip, axis, other(4, 2)).astype(f32)
    return both, lax.ppermute(both, axis, other(4, 1))


def after(x, *others):
    return lax.optimization_barrier((x,) + others)[0]


def right_sum(make, finish, chunks, axis):
    count = len(chunks)
    sent = [None] * count
    halves = [None] * count
    totals = [None] * count
    backs = [None] * count
    token = None

    def part(k):
        nonlocal token
        sent[k] = make(k, token)
        token = sent[k]

    def half(k):
        nonlocal token
        came = lax.ppermute(sent[k], axis, [(0, 1), (3, 2)])
        mine = after(sent[k], token)
        token = halves[k] = (mine.astype(f32) + came.astype(f32)).astype(mine.dtype)

    def total(k):
        nonlocal token
        across = lax.ppermute(halves[k], axis, [(1, 2), (2, 1)])
        mine = after(halves[k], token)
        token = totals[k] = (mine.astype(f32) + across.astype(f32)).astype(mine.dtype)

    def back(k):
        nonlocal token
        backs[k] = lax.ppermute(totals[k], axis, [(1, 0), (2, 3)])
        token = finish(k, totals[k], backs[k], token)

    for name, k in ORDER:
        (part, half, total, back)["phtv".index(name)](k)


def body(activations, out_grads, matrix, left, right):
    col_count = lax.axis_size("col")
    row_count = lax.axis_size("row")
    m, n = matrix.shape
    shard = out_grads.shape[0]
    line = row_count == 4 and col_count == 4
    twice = jnp.concatenate([right, right], axis=1)
    prev = None
    if line:
        outward = [(0, 1), (1, 0), (2, 3), (3, 2)]
        across = [(1, 2), (2, 1)]
        onward = [(1, 0), (2, 3)]
        outer = lax.ppermute(out_grads, "row", outward)
        inner = lax.ppermute(out_grads, "row", across)
        chunks = cut(n, FIRST)
        outers = [lax.slice_in_dim(outer, o, o + k, axis=1) for o, k in chunks]
        inners = [lax.slice_in_dim(inner, o, o + k, axis=1) for o, k in chunks]
        beside = lax.ppermute(activations, "col", other(4, 1))
        beyond = lax.ppermute(activations, "col", other(4, 2))
        crossed = [lax.ppermute(after(outers[0], beside, beyond), "row", across)]
        crossed += [lax.ppermute(after(x, crossed[0]), "row", across) for x in outers[1:]]
        corner = lax.ppermute(after(beyond, crossed[0]), "col", other(4, 1))
        blocks = jnp.stack([activations, beside, beyond, corner])
        me = lax.axis_index("col")
        ordered = jnp.concatenate([lax.dynamic_index_in_dim(blocks, k ^ me, 0, False) for k in line_order("row")], axis=0)
        at = ordered.T
        partials = []
        for k, (offset, width) in enumerate(chunks):
            if k == 0:
                early = lax.ppermute(inners[0], "row", onward)
                late = lax.ppermute(after(crossed[0], early), "row", onward)
                ends = [(early, shard, 0, False), (late, shard, 0, False)]
            else:
                both = jnp.concatenate([inners[k], crossed[k]], axis=0)
                both = after(both, at if k == 1 else partials[k - 2])
                end = lax.ppermute(both, "row", onward)
                ends = [(end, shard, 0, False), (end, shard, 1, False)]
            groups = [[(out_grads, shard, 0, True)], [(outer, shard, 0, True)],
                      [(inner, shard, 0, True), ends[0]], [(crossed[k], shard, 0, False), ends[1]]]
            prev = first_pass(at, matrix, left, right, groups, offset, width, prev, BLOCK, TILE)
            partials.append(prev[1])
    else:
        gathered = lax.all_gather(activations, "col", axis=0, tiled=True)
        grads = lax.all_gather(out_grads, "row", axis=0, tiled=True)
        prev = first_pass(gathered.T, matrix, left, right, [[(grads, grads.shape[0], 0, True)]], 0, n, None, BLOCK, TILE)
    fisher, partial = prev
    halves = sum_columns(partial, "col")
    side = lax.axis_index("col") & 1 if col_count == 4 else 0
    sums, left_descent = left_curve(jnp.full((1, 1), side, jnp.int32), halves, right, fisher)
    pieces = pieces_of(add_up(sums, "col"), "row")
    step, left_new, new_t, pair = left_update(left, left_descent, pieces, col_count)
    central = (lax.axis_index("row") % 3 != 0) if line else True
    flag = jnp.full((1, 1), central, jnp.int32)
    chunks = cut(n, SECOND)
    sums = jnp.zeros((2, 8, 128), f32)
    parts = [None] * len(chunks)

    def make(k, token):
        return partial_pass(pair, matrix, twice, fisher, new_t, step if token is None else token, *chunks[k])

    def finish(k, total, back, token):
        nonlocal sums
        if token is not None:
            total = after(total, token)
        sums, parts[k] = right_curve(flag, left_new, total, back, fisher, sums, *chunks[k])
        return sums

    if line:
        right_sum(make, finish, chunks, "row")
    else:
        for k in range(len(chunks)):
            total = lax.psum(make(k, None), "row")
            finish(k, total, total, None)
    pieces = pieces_of(add_up(sums, "col"), "row")
    residual, right_new = last_pass(matrix, pair, twice, left_new, parts, pieces, row_count)
    return (left_new, right_new, residual)


def solution(mesh):
    placed = (
        P(("grp", "col"), "row"),
        P(("grp", "row"), "col"),
        P(("grp", "row"), "col"),
        P(("grp", "row"), None),
        P(("grp", "col"), None),
    )
    return jax.shard_map(
        body,
        mesh=mesh,
        in_specs=placed,
        out_specs=(P(("grp", "row"), None), P(("grp", "col"), None), P(("grp", "row"), "col")),
        check_vma=False,
    )
```

profile of v0, /device:TPU:0, one launch (start us, length us, event | category | flops | bytes accessed | tf_op | source)
XLA Modules:
  0.0 270.1 jit_solution(8406440727094711265)
XLA Ops:
  0.6 3.1 %collective-permute-start.2 = (bf16[128,4608]{1,0:T(8,128)(2,1)}, bf16[128,4608]{1,0:T(8,128)(2,1)S(1)}, u32[]{:S(2)}, u32[]{:S(2)}) collective-permute-start(bf16[128,4608]{1,0:T(8,128)(2,1)} %refs_4_.5), channel_id=1, source_target_pairs={{0,4},{4,0},{8,12},{12,8},{1,5},{5,1},{9,13},{13,9},{2,6},{6,2},{1... | collective-permute-start | bytes 3538952 | tf_op jit(solution)/shard_map/ppermute | solution.py:476
  3.7 0.7 collective-permute-start.5
  4.5 1.6 collective-permute-start.1
  6.0 23.9 %collective-permute-done.2.refs_5_ = bf16[128,4608]{1,0:T(8,128)(2,1)S(1)} collective-permute-done((bf16[128,4608]{1,0:T(8,128)(2,1)}, bf16[128,4608]{1,0:T(8,128)(2,1)S(1)}, u32[]{:S(2)}, u32[]{:S(2)}) %collective-permute-start.2) | collective-permute-done | bytes 1179680 | tf_op jit(solution)/shard_map/ppermute | solution.py:476
  30.0 1.6 collective-permute-start.3
  31.7 1.3 collective-permute-start.7
  33.1 0.8 slice.29
  34.6 14.4 %collective-permute-done.7.refs_7_ = bf16[128,2304]{1,0:T(8,128)(2,1)} collective-permute-done((bf16[128,2304]{1,0:T(8,128)(2,1)S(1)}, bf16[128,2304]{1,0:T(8,128)(2,1)}, u32[]{:S(2)}, u32[]{:S(2)}) %collective-permute-start.7) | collective-permute-done | bytes 589856 | tf_op jit(solution)/shard_map/ppermute | solution.py:493
  49.0 1.3 collective-permute-start.8
  51.0 1.3 pad_maximum_fusion
  53.6 0.8 slice-done.1
  54.4 1.3 collective-permute-start.11
  55.8 11.8 %collective-permute-done.8.refs_9_ = bf16[128,2304]{1,0:T(8,128)(2,1)S(1)} collective-permute-done((bf16[128,2304]{1,0:T(8,128)(2,1)}, bf16[128,2304]{1,0:T(8,128)(2,1)S(1)}, u32[]{:S(2)}, u32[]{:S(2)}) %collective-permute-start.8) | collective-permute-done | bytes 589856 | tf_op jit(solution)/shard_map/ppermute | solution.py:494
  67.6 0.8 copy-done.11
  68.4 12.7 %first_pass.3 = (bf16[1536,4608]{1,0:T(8,128)(2,1)}, f32[1536,256]{1,0:T(8,128)S(1)}) custom-call(bf16[1536,512]{1,0:T(8,128)(2,1)S(1)} %maximum_bitcast_fusion.refs_0_, bf16[1536,4608]{1,0:T(8,128)(2,1)} %refs_0_.3, bf16[1536,256]{1,0:T(8,128)(2,1)} %refs_0_.2, bf16[4608,256]{1,0:T(8,128)(2,1)} %r_ref.1, bf16[128,4608]{1,0:T(8,128)(2,1)} %refs_4_.5, ...), custom_call_target="tpu_custom_call" | custom-call | flops 7247757312 | bytes 14155776 | tf_op jit(solution)/shard_map/first_pass/pallas_call | solution.py:129
  81.1 1.5 collective-permute-start.9
  82.6 3.0 %collective-permute-done.11.refs_7_.refs_9_ = bf16[256,1536]{1,0:T(8,128)(2,1)S(1)} collective-permute-done((bf16[256,1536]{1,0:T(8,128)(2,1)S(1)}, bf16[256,1536]{1,0:T(8,128)(2,1)S(1)}, u32[]{:S(2)}, u32[]{:S(2)}) %collective-permute-start.11) | collective-permute-done | bytes 786464 | tf_op jit(solution)/shard_map/ppermute | solution.py:499
  85.6 0.9 copy-done.4
  86.5 10.7 %first_pass.4 = (bf16[1536,4608]{1,0:T(8,128)(2,1)}, f32[1536,256]{1,0:T(8,128)S(1)}) custom-call(bf16[1536,512]{1,0:T(8,128)(2,1)S(1)} %maximum_bitcast_fusion.refs_0_, bf16[1536,4608]{1,0:T(8,128)(2,1)} %refs_0_.3, bf16[1536,256]{1,0:T(8,128)(2,1)} %refs_0_.2, bf16[4608,256]{1,0:T(8,128)(2,1)} %r_ref.1, ...), custom_call_target="tpu_custom_call", output_to_operand_aliasing={{1}: (10, {}), {0}: (11, {})} | custom-call | flops 4831838208 | bytes 9437184 | tf_op jit(solution)/shard_map/first_pass/pallas_call | solution.py:129
  97.2 0.7 copy-done.5
  98.0 6.1 %first_pass.5 = (bf16[1536,4608]{1,0:T(8,128)(2,1)}, f32[1536,256]{1,0:T(8,128)S(1)}) custom-call(bf16[1536,512]{1,0:T(8,128)(2,1)S(1)} %maximum_bitcast_fusion.refs_0_, bf16[1536,4608]{1,0:T(8,128)(2,1)} %refs_0_.3, bf16[1536,256]{1,0:T(8,128)(2,1)} %refs_0_.2, bf16[4608,256]{1,0:T(8,128)(2,1)} %r_ref.1, ...), custom_call_target="tpu_custom_call", output_to_operand_aliasing={{1}: (10, {}), {0}: (11, {})} | custom-call | flops 2415919104 | bytes 4718592 | tf_op jit(solution)/shard_map/first_pass/pallas_call | solution.py:129
  104.2 2.3 collective-permute-done.12
  106.5 1.6 collective-permute-start.13
  108.1 9.7 %collective-permute-done.13 = bf16[768,256]{1,0:T(8,128)(2,1)S(1)} collective-permute-done((bf16[768,256]{1,0:T(8,128)(2,1)S(1)}, bf16[768,256]{1,0:T(8,128)(2,1)S(1)}, u32[]{:S(2)}, u32[]{:S(2)}) %collective-permute-start.13) | collective-permute-done | bytes 393248 | tf_op jit(solution)/shard_map/ppermute | solution.py:422
  117.9 2.3 collective-permute-done.14.c_ref
  120.2 8.5 %left_curve.1 = (f32[2,8,128]{2,1,0:T(8,128)S(1)}, f32[1536,256]{1,0:T(8,128)S(1)}) custom-call(s32[1,1]{1,0:T(1,128)} %bitcast.side_ref, f32[768,256]{1,0:T(8,128)S(1)} %convert_add_fusion.b_ref, f32[768,256]{1,0:T(8,128)S(1)} %collective-permute-done.14.c_ref, bf16[4608,256]{1,0:T(8,128)(2,1)} %r_ref.1, bf16[1536,4608]{1,0:T(8,128)(2,1)} %get-tuple-element.56.f_ref), custom_call_target="tpu_custom_call" | custom-call | flops 3623878656 | bytes 14155776 | tf_op jit(solution)/shard_map/left_curve/pallas_call | solution.py:183
  128.9 1.6 collective-permute-start.17
  130.5 1.5 collective-permute-start.15
  132.3 1.9 collective-permute-done.15
  134.2 3.5 %collective-permute-start.19 = (f32[2,8,128]{2,1,0:T(8,128)S(1)}, f32[2,8,128]{2,1,0:T(8,128)S(1)}, u32[]{:S(2)}, u32[]{:S(2)}) collective-permute-start(f32[2,8,128]{2,1,0:T(8,128)S(1)} %add_add_fusion.1.refs_2_), channel_id=1, source_target_pairs={{0,8},{4,12},{8,0},{12,4},{1,9},{5,13},{9,1},{13,5},{2,10},{6,14},... | collective-permute-start | bytes 24584 | tf_op jit(solution)/shard_map/ppermute | solution.py:388
  138.4 1.3 collective-permute-done.18.refs_3_
  139.7 1.7 collective-permute-done.20.refs_5_
  141.4 2.8 %left_update.1 = (f32[8,128]{1,0:T(8,128)S(1)}, bf16[1536,256]{1,0:T(8,128)(2,1)}, bf16[256,1536]{1,0:T(8,128)(2,1)S(1)}, bf16[1536,512]{1,0:T(8,128)(2,1)S(1)}) custom-call(bf16[1536,256]{1,0:T(8,128)(2,1)} %refs_0_.2, f32[1536,256]{1,0:T(8,128)S(1)} %get-tuple-element.57.refs_1_, f32[2,8,128]{2,1,0:T(8,128)S(1)} %add_add_fusion.1.refs_2_, ...), custom_call_target="tpu_custom_call" | custom-call | flops 786432 | bytes 3932160 | tf_op jit(solution)/shard_map/left_update/pallas_call | solution.py:254
  144.2 6.4 %partial_pass.4.k_ref = bf16[256,1152]{1,0:T(8,128)(2,1)S(1)} custom-call(bf16[1536,512]{1,0:T(8,128)(2,1)S(1)} %get-tuple-element.60.p_ref.refs_1_, bf16[1536,4608]{1,0:T(8,128)(2,1)} %refs_0_.3, bf16[4608,512]{1,0:T(8,128)(2,1)} %copy-done, bf16[1536,4608]{1,0:T(8,128)(2,1)} %get-tuple-element.56.f_ref, bf16[256,1536]{1,0:T(8,128)(2,1)S(1)} %get-tuple-element.61.t_ref, ...), custom_call_target="tpu_custom_call" | custom-call | flops 2717908992 | bytes 7077888 | tf_op jit(solution)/shard_map/partial_pass/pallas_call | solution.py:285
  150.6 3.0 %collective-permute-start.21 = (bf16[256,1152]{1,0:T(8,128)(2,1)S(1)}, bf16[256,1152]{1,0:T(8,128)(2,1)S(1)}, u32[]{:S(2)}, u32[]{:S(2)}) collective-permute-start(bf16[256,1152]{1,0:T(8,128)(2,1)S(1)} %partial_pass.4.k_ref), channel_id=1, source_target_pairs={{0,4},{12,8},{1,5},{13,9},{2,6},{14,10},{3,7},{15,11},{16,20},{28,... | collective-permute-start | bytes 1769480 | tf_op jit(solution)/shard_map/ppermute | solution.py:445
  153.6 6.4 %partial_pass.5.k_ref = bf16[256,1152]{1,0:T(8,128)(2,1)S(1)} custom-call(bf16[1536,512]{1,0:T(8,128)(2,1)S(1)} %get-tuple-element.60.p_ref.refs_1_, bf16[1536,4608]{1,0:T(8,128)(2,1)} %refs_0_.3, bf16[4608,512]{1,0:T(8,128)(2,1)} %copy-done, bf16[1536,4608]{1,0:T(8,128)(2,1)} %get-tuple-element.56.f_ref, bf16[256,1536]{1,0:T(8,128)(2,1)S(1)} %get-tuple-element.61.t_ref, ...), custom_call_target="tpu_custom_call" | custom-call | flops 2717908992 | bytes 7077888 | tf_op jit(solution)/shard_map/partial_pass/pallas_call | solution.py:285
  160.0 1.3 collective-permute-start.22
  161.4 6.4 %partial_pass.6 = bf16[256,1152]{1,0:T(8,128)(2,1)S(1)} custom-call(bf16[1536,512]{1,0:T(8,128)(2,1)S(1)} %get-tuple-element.60.p_ref.refs_1_, bf16[1536,4608]{1,0:T(8,128)(2,1)} %refs_0_.3, bf16[4608,512]{1,0:T(8,128)(2,1)} %copy-done, bf16[1536,4608]{1,0:T(8,128)(2,1)} %get-tuple-element.56.f_ref, bf16[256,1536]{1,0:T(8,128)(2,1)S(1)} %get-tuple-element.61.t_ref, ...), custom_call_target="tpu_custom_call" | custom-call | flops 2717908992 | bytes 7077888 | tf_op jit(solution)/shard_map/partial_pass/pallas_call | solution.py:285
  167.8 1.3 collective-permute-start.24
  169.3 0.7 collective-permute-start.23
  170.0 6.4 %partial_pass.7 = bf16[256,1152]{1,0:T(8,128)(2,1)S(1)} custom-call(bf16[1536,512]{1,0:T(8,128)(2,1)S(1)} %get-tuple-element.60.p_ref.refs_1_, bf16[1536,4608]{1,0:T(8,128)(2,1)} %refs_0_.3, bf16[4608,512]{1,0:T(8,128)(2,1)} %copy-done, bf16[1536,4608]{1,0:T(8,128)(2,1)} %get-tuple-element.56.f_ref, bf16[256,1536]{1,0:T(8,128)(2,1)S(1)} %get-tuple-element.61.t_ref, ...), custom_call_target="tpu_custom_call" | custom-call | flops 2717908992 | bytes 7077888 | tf_op jit(solution)/shard_map/partial_pass/pallas_call | solution.py:285
  176.4 4.2 %collective-permute-start.26 = (bf16[256,1152]{1,0:T(8,128)(2,1)S(1)}, bf16[256,1152]{1,0:T(8,128)(2,1)S(1)}, u32[]{:S(2)}, u32[]{:S(2)}) collective-permute-start(bf16[256,1152]{1,0:T(8,128)(2,1)S(1)} %partial_pass.7), channel_id=1, source_target_pairs={{0,4},{12,8},{1,5},{13,9},{2,6},{14,10},{3,7},{15,11},{16,20},{28,... | collective-permute-start | bytes 1769480 | tf_op jit(solution)/shard_map/ppermute | solution.py:445
  180.8 0.7 collective-permute-start.25
  181.7 1.3 collective-permute-start.27
  183.0 9.4 %collective-permute-done.24 = bf16[256,1152]{1,0:T(8,128)(2,1)S(1)} collective-permute-done((bf16[256,1152]{1,0:T(8,128)(2,1)S(1)}, bf16[256,1152]{1,0:T(8,128)(2,1)S(1)}, u32[]{:S(2)}, u32[]{:S(2)}) %collective-permute-start.24) | collective-permute-done | bytes 589856 | tf_op jit(solution)/shard_map/ppermute | solution.py:445
  192.5 0.7 collective-permute-start.28
  193.4 1.3 collective-permute-start.29
  194.7 7.2 %collective-permute-done.26 = bf16[256,1152]{1,0:T(8,128)(2,1)S(1)} collective-permute-done((bf16[256,1152]{1,0:T(8,128)(2,1)S(1)}, bf16[256,1152]{1,0:T(8,128)(2,1)S(1)}, u32[]{:S(2)}, u32[]{:S(2)}) %collective-permute-start.26) | collective-permute-done | bytes 589856 | tf_op jit(solution)/shard_map/ppermute | solution.py:445
  202.8 3.6 %right_curve.4 = (f32[2,8,128]{2,1,0:T(8,128)S(1)}, bf16[256,1152]{1,0:T(8,128)(2,1)S(1)}) custom-call(s32[1,1]{1,0:T(1,128)} %bitcast.10.flag_ref, bf16[1536,256]{1,0:T(8,128)(2,1)} %get-tuple-element.41.a_ref.refs_3_, bf16[256,1152]{1,0:T(8,128)(2,1)S(1)} %add_convert_fusion.5.t_ref, bf16[256,1152]{1,0:T(8,128)(2,1)S(1)} %collective-permute-done.27.b_ref, ...), custom_call_target="tpu_custom_call" | custom-call | flops 905969664 | bytes 3538944 | tf_op jit(solution)/shard_map/right_curve/pallas_call | solution.py:222
  206.5 1.3 collective-permute-start.31
  208.4 3.6 %right_curve.5 = (f32[2,8,128]{2,1,0:T(8,128)S(1)}, bf16[256,1152]{1,0:T(8,128)(2,1)S(1)}) custom-call(s32[1,1]{1,0:T(1,128)} %bitcast.10.flag_ref, bf16[1536,256]{1,0:T(8,128)(2,1)} %get-tuple-element.41.a_ref.refs_3_, bf16[256,1152]{1,0:T(8,128)(2,1)S(1)} %add_convert_fusion.3.t_ref, bf16[256,1152]{1,0:T(8,128)(2,1)S(1)} %collective-permute-done.29.b_ref, ...), custom_call_target="tpu_custom_call" | custom-call | flops 905969664 | bytes 3538944 | tf_op jit(solution)/shard_map/right_curve/pallas_call | solution.py:222
  212.2 1.3 collective-permute-start.32
  213.5 10.4 %collective-permute-done.31.b_ref = bf16[256,1152]{1,0:T(8,128)(2,1)S(1)} collective-permute-done((bf16[256,1152]{1,0:T(8,128)(2,1)S(1)}, bf16[256,1152]{1,0:T(8,128)(2,1)S(1)}, u32[]{:S(2)}, u32[]{:S(2)}) %collective-permute-start.31) | collective-permute-done | bytes 589856 | tf_op jit(solution)/shard_map/ppermute | solution.py:457
  223.9 3.6 %right_curve.6 = (f32[2,8,128]{2,1,0:T(8,128)S(1)}, bf16[256,1152]{1,0:T(8,128)(2,1)S(1)}) custom-call(s32[1,1]{1,0:T(1,128)} %bitcast.10.flag_ref, bf16[1536,256]{1,0:T(8,128)(2,1)} %get-tuple-element.41.a_ref.refs_3_, bf16[256,1152]{1,0:T(8,128)(2,1)S(1)} %add_convert_fusion.1.t_ref, bf16[256,1152]{1,0:T(8,128)(2,1)S(1)} %collective-permute-done.31.b_ref, ...), custom_call_target="tpu_custom_call" | custom-call | flops 905969664 | bytes 3538944 | tf_op jit(solution)/shard_map/right_curve/pallas_call | solution.py:222
  227.5 7.7 %collective-permute-done.32.b_ref = bf16[256,1152]{1,0:T(8,128)(2,1)S(1)} collective-permute-done((bf16[256,1152]{1,0:T(8,128)(2,1)S(1)}, bf16[256,1152]{1,0:T(8,128)(2,1)S(1)}, u32[]{:S(2)}, u32[]{:S(2)}) %collective-permute-start.32) | collective-permute-done | bytes 589856 | tf_op jit(solution)/shard_map/ppermute | solution.py:457
  235.2 3.6 %right_curve.7 = (f32[2,8,128]{2,1,0:T(8,128)S(1)}, bf16[256,1152]{1,0:T(8,128)(2,1)S(1)}) custom-call(s32[1,1]{1,0:T(1,128)} %bitcast.10.flag_ref, bf16[1536,256]{1,0:T(8,128)(2,1)} %get-tuple-element.41.a_ref.refs_3_, bf16[256,1152]{1,0:T(8,128)(2,1)S(1)} %add_convert_fusion.t_ref, bf16[256,1152]{1,0:T(8,128)(2,1)S(1)} %collective-permute-done.32.b_ref, ...), custom_call_target="tpu_custom_call" | custom-call | flops 905969664 | bytes 3538944 | tf_op jit(solution)/shard_map/right_curve/pallas_call | solution.py:222
  238.9 1.7 collective-permute-start.35
  240.6 1.3 collective-permute-done.34
  242.0 2.3 collective-permute-done.33
  244.3 2.7 collective-permute-start.37
  246.9 1.2 collective-permute-start.38
  248.1 1.6 collective-permute-done.36.refs_9_
  249.7 0.9 collective-permute-done.38.refs_11_
  250.6 19.5 %last_pass.1 = (bf16[1536,4608]{1,0:T(8,128)(2,1)}, bf16[4608,256]{1,0:T(8,128)(2,1)}) custom-call(bf16[1536,4608]{1,0:T(8,128)(2,1)} %refs_0_.3, bf16[1536,512]{1,0:T(8,128)(2,1)S(1)} %get-tuple-element.60.p_ref.refs_1_, bf16[4608,512]{1,0:T(8,128)(2,1)} %copy-done, bf16[1536,256]{1,0:T(8,128)(2,1)} %get-tuple-element.41.a_ref.refs_3_, ...), custom_call_target="tpu_custom_call" | custom-call | flops 10871635968 | bytes 28311552 | tf_op jit(solution)/shard_map/last_pass/pallas_call | solution.py:343
  (85 shorter events, 6.8 us)
Async XLA Ops:
  0.6 29.3 %collective-permute-start.2 = (bf16[128,4608]{1,0:T(8,128)(2,1)}, bf16[128,4608]{1,0:T(8,128)(2,1)S(1)}, u32[]{:S(2)}, u32[]{:S(2)}) collective-permute-start(bf16[128,4608]{1,0:T(8,128)(2,1)} %refs_4_.5), channel_id=1, source_target_pairs={{0,4},{4,0},{8,12},{12,8},{1,5},{5,1},{9,13},{13,9},{2,6},{6,2},{1... | collective-permute-start | bytes 3538952 | tf_op jit(solution)/shard_map/ppermute | solution.py:476
  3.7 27.9 %collective-permute-start.5 = (bf16[128,4608]{1,0:T(8,128)(2,1)}, bf16[128,4608]{1,0:T(8,128)(2,1)S(1)}, u32[]{:S(2)}, u32[]{:S(2)}) collective-permute-start(bf16[128,4608]{1,0:T(8,128)(2,1)} %refs_4_.5), channel_id=1, source_target_pairs={{4,8},{8,4},{5,9},{9,5},{6,10},{10,6},{7,11},{11,7},{20,24},{24,20... | collective-permute-start | bytes 3538952 | tf_op jit(solution)/shard_map/ppermute | solution.py:477
  4.5 25.5 %collective-permute-start.1 = (bf16[128,1536]{1,0:T(8,128)(2,1)}, bf16[128,1536]{1,0:T(8,128)(2,1)}, u32[]{:S(2)}, u32[]{:S(2)}) collective-permute-start(bf16[128,1536]{1,0:T(8,128)(2,1)} %param.5), channel_id=1, source_target_pairs={{0,2},{1,3},{2,0},{3,1},{4,6},{5,7},{6,4},{7,5},{8,10},{9,11},{10,... | collective-permute-start | bytes 1179656 | tf_op jit(solution)/shard_map/ppermute | solution.py:482
  6.0 24.0 %collective-permute-start = (bf16[128,1536]{1,0:T(8,128)(2,1)}, bf16[128,1536]{1,0:T(8,128)(2,1)S(1)}, u32[]{:S(2)}, u32[]{:S(2)}) collective-permute-start(bf16[128,1536]{1,0:T(8,128)(2,1)} %param.5), channel_id=1, source_target_pairs={{0,1},{1,0},{2,3},{3,2},{4,5},{5,4},{6,7},{7,6},{8,9},{9,8},{10,11... | collective-permute-start | bytes 1179656 | tf_op jit(solution)/shard_map/ppermute | solution.py:481
  29.9 3.2 %copy-start.2 = (bf16[128,4608]{1,0:T(8,128)(2,1)}, bf16[128,4608]{1,0:T(8,128)(2,1)S(1)}, u32[]{:S(2)}) copy-start(bf16[128,4608]{1,0:T(8,128)(2,1)S(1)} %collective-permute-done.2.refs_5_) | copy-start | bytes 3538948
  29.9 21.0 %copy-start.8 = (bf16[128,1536]{1,0:T(8,128)(2,1)S(1)}, bf16[128,1536]{1,0:T(8,128)(2,1)}, u32[]{:S(2)}) copy-start(bf16[128,1536]{1,0:T(8,128)(2,1)} %param.5) | copy-start | bytes 1179652
  30.0 3.0 %copy-start.9 = (bf16[128,1536]{1,0:T(8,128)(2,1)}, bf16[128,1536]{1,0:T(8,128)(2,1)S(1)}, u32[]{:S(2)}) copy-start(bf16[128,1536]{1,0:T(8,128)(2,1)S(1)} %collective-permute-done) | copy-start | bytes 1179652
  30.0 3.0 %collective-permute-start.3 = (bf16[128,2304]{1,0:T(8,128)(2,1)S(1)}, bf16[128,2304]{1,0:T(8,128)(2,1)}, u32[]{:S(2)}, u32[]{:S(2)}) collective-permute-start(bf16[128,2304]{1,0:T(8,128)(2,1)S(1)} %slice.24), channel_id=1, source_target_pairs={{4,8},{8,4},{5,9},{9,5},{6,10},{10,6},{7,11},{11,7},{20,24},{24,20... | collective-permute-start | bytes 1769480 | tf_op jit(solution)/shard_map/ppermute | solution.py:483
  31.6 2.3 copy-start.3
  31.7 17.3 %collective-permute-start.7 = (bf16[128,2304]{1,0:T(8,128)(2,1)S(1)}, bf16[128,2304]{1,0:T(8,128)(2,1)}, u32[]{:S(2)}, u32[]{:S(2)}) collective-permute-start(bf16[128,2304]{1,0:T(8,128)(2,1)S(1)} %slice.27), channel_id=1, source_target_pairs={{4,0},{8,12},{5,1},{9,13},{6,2},{10,14},{7,3},{11,15},{20,16},{24,... | collective-permute-start | bytes 1769480 | tf_op jit(solution)/shard_map/ppermute | solution.py:493
  33.0 18.0 %collective-permute-start.4 = (bf16[128,1536]{1,0:T(8,128)(2,1)}, bf16[128,1536]{1,0:T(8,128)(2,1)}, u32[]{:S(2)}, u32[]{:S(2)}) collective-permute-start(bf16[128,1536]{1,0:T(8,128)(2,1)} %collective-permute-done.1), channel_id=1, source_target_pairs={{0,1},{1,0},{2,3},{3,2},{4,5},{5,4},{6,7},{7,6},{8,9},{9,8},{10,11... | collective-permute-start | bytes 1179656 | tf_op jit(solution)/shard_map/ppermute | solution.py:485
  33.1 17.9 %copy-start.10 = (bf16[128,1536]{1,0:T(8,128)(2,1)S(1)}, bf16[128,1536]{1,0:T(8,128)(2,1)}, u32[]{:S(2)}) copy-start(bf16[128,1536]{1,0:T(8,128)(2,1)} %copy-done.9) | copy-start | bytes 1179652
  33.9 21.8 %collective-permute-start.6 = (bf16[128,768]{1,0:T(8,128)(2,1)S(1)}, bf16[128,768]{1,0:T(8,128)(2,1)S(1)}, u32[]{:S(2)}, u32[]{:S(2)}) collective-permute-start(bf16[128,768]{1,0:T(8,128)(2,1)S(1)} %slice.26), channel_id=1, source_target_pairs={{4,8},{8,4},{5,9},{9,5},{6,10},{10,6},{7,11},{11,7},{20,24},{24,20... | collective-permute-start | bytes 589832 | tf_op jit(solution)/shard_map/ppermute | solution.py:484
  49.0 18.6 %collective-permute-start.8 = (bf16[128,2304]{1,0:T(8,128)(2,1)}, bf16[128,2304]{1,0:T(8,128)(2,1)S(1)}, u32[]{:S(2)}, u32[]{:S(2)}) collective-permute-start(bf16[128,2304]{1,0:T(8,128)(2,1)} %collective-permute-done.3.refs_8_), channel_id=1, source_target_pairs={{4,0},{8,12},{5,1},{9,13},{6,2},{10,14},{7,3},{11,15},{20,16},{24,... | collective-permute-start | bytes 1769480 | tf_op jit(solution)/shard_map/ppermute | solution.py:494
  50.3 3.3 %collective-permute-start.10 = (bf16[128,1536]{1,0:T(8,128)(2,1)}, bf16[128,1536]{1,0:T(8,128)(2,1)S(1)}, u32[]{:S(2)}, u32[]{:S(2)}) collective-permute-start(bf16[128,1536]{1,0:T(8,128)(2,1)} %slice.29), channel_id=1, source_target_pairs={{4,8},{8,4},{5,9},{9,5},{6,10},{10,6},{7,11},{11,7},{20,24},{24,20... | collective-permute-start | bytes 1179656 | tf_op jit(solution)/shard_map/ppermute | solution.py:484
  53.3 1.0 slice-start.1
  53.4 2.4 slice-start
  54.3 26.7 %copy-start.6 = (bf16[128,1536]{1,0:T(8,128)(2,1)}, bf16[128,1536]{1,0:T(8,128)(2,1)S(1)}, u32[]{:S(2)}) copy-start(bf16[128,1536]{1,0:T(8,128)(2,1)S(1)} %collective-permute-done.10.refs_8_) | copy-start | bytes 1179652
  54.4 31.2 %collective-permute-start.11 = (bf16[256,1536]{1,0:T(8,128)(2,1)S(1)}, bf16[256,1536]{1,0:T(8,128)(2,1)S(1)}, u32[]{:S(2)}, u32[]{:S(2)}) collective-permute-start(bf16[256,1536]{1,0:T(8,128)(2,1)S(1)} %pad_maximum_fusion.1), channel_id=1, source_target_pairs={{4,0},{8,12},{5,1},{9,13},{6,2},{10,14},{7,3},{11,15},{20,16},{24,... | collective-permute-start | bytes 2359304 | tf_op jit(solution)/shard_map/ppermute | solution.py:499
  55.7 25.4 %copy-start.7 = (bf16[128,768]{1,0:T(8,128)(2,1)}, bf16[128,768]{1,0:T(8,128)(2,1)S(1)}, u32[]{:S(2)}) copy-start(bf16[128,768]{1,0:T(8,128)(2,1)S(1)} %collective-permute-done.6.refs_8_) | copy-start | bytes 589828
  67.6 0.8 copy-start.11
  81.1 16.1 %collective-permute-start.9 = (bf16[256,768]{1,0:T(8,128)(2,1)S(1)}, bf16[256,768]{1,0:T(8,128)(2,1)S(1)}, u32[]{:S(2)}, u32[]{:S(2)}) collective-permute-start(bf16[256,768]{1,0:T(8,128)(2,1)S(1)} %pad_maximum_fusion.2), channel_id=1, source_target_pairs={{4,0},{8,12},{5,1},{9,13},{6,2},{10,14},{7,3},{11,15},{20,16},{24,... | collective-permute-start | bytes 1179656 | tf_op jit(solution)/shard_map/ppermute | solution.py:499
  85.6 0.9 copy-start.4
  97.2 0.7 copy-start.5
  104.1 2.4 collective-permute-start.12
  106.5 11.2 %collective-permute-start.13 = (bf16[768,256]{1,0:T(8,128)(2,1)S(1)}, bf16[768,256]{1,0:T(8,128)(2,1)S(1)}, u32[]{:S(2)}, u32[]{:S(2)}) collective-permute-start(bf16[768,256]{1,0:T(8,128)(2,1)S(1)} %add_convert_fusion.8), channel_id=1, source_target_pairs={{0,2},{1,3},{2,0},{3,1},{4,6},{5,7},{6,4},{7,5},{8,10},{9,11},{10,... | collective-permute-start | bytes 1179656 | tf_op jit(solution)/shard_map/ppermute | solution.py:422
  117.9 2.4 collective-permute-start.14
  120.2 11.8 %copy-start.1 = (bf16[4608,256]{1,0:T(8,128)(2,1)S(1)}, bf16[4608,256]{1,0:T(8,128)(2,1)}, u32[]{:S(2)}) copy-start(bf16[4608,256]{1,0:T(8,128)(2,1)} %r_ref.1) | copy-start | bytes 7077892
  128.8 3.5 %collective-permute-start.16 = (f32[2,8,128]{2,1,0:T(8,128)S(1)}, f32[2,8,128]{2,1,0:T(8,128)S(1)}, u32[]{:S(2)}, u32[]{:S(2)}) collective-permute-start(f32[2,8,128]{2,1,0:T(8,128)S(1)} %get-tuple-element.58), channel_id=1, source_target_pairs={{0,1},{1,2},{2,3},{3,0},{4,5},{5,6},{6,7},{7,4},{8,9},{9,10},{10,1... | collective-permute-start | bytes 24584 | tf_op jit(solution)/shard_map/ppermute | solution.py:388
  128.9 3.3 %collective-permute-start.17 = (f32[2,8,128]{2,1,0:T(8,128)S(1)}, f32[2,8,128]{2,1,0:T(8,128)S(1)}, u32[]{:S(2)}, u32[]{:S(2)}) collective-permute-start(f32[2,8,128]{2,1,0:T(8,128)S(1)} %get-tuple-element.58), channel_id=1, source_target_pairs={{0,3},{1,0},{2,1},{3,2},{4,7},{5,4},{6,5},{7,6},{8,11},{9,8},{10,9... | collective-permute-start | bytes 24584 | tf_op jit(solution)/shard_map/ppermute | solution.py:388
  130.5 3.7 %collective-permute-start.15 = (f32[2,8,128]{2,1,0:T(8,128)S(1)}, f32[2,8,128]{2,1,0:T(8,128)S(1)}, u32[]{:S(2)}, u32[]{:S(2)}) collective-permute-start(f32[2,8,128]{2,1,0:T(8,128)S(1)} %get-tuple-element.58), channel_id=1, source_target_pairs={{0,2},{1,3},{2,0},{3,1},{4,6},{5,7},{6,4},{7,5},{8,10},{9,11},{10,... | collective-permute-start | bytes 24584 | tf_op jit(solution)/shard_map/ppermute | solution.py:388
  134.2 5.4 %collective-permute-start.18 = (f32[2,8,128]{2,1,0:T(8,128)S(1)}, f32[2,8,128]{2,1,0:T(8,128)S(1)}, u32[]{:S(2)}, u32[]{:S(2)}) collective-permute-start(f32[2,8,128]{2,1,0:T(8,128)S(1)} %add_add_fusion.1.refs_2_), channel_id=1, source_target_pairs={{0,4},{4,8},{8,12},{12,0},{1,5},{5,9},{9,13},{13,1},{2,6},{6,10},{... | collective-permute-start | bytes 24584 | tf_op jit(solution)/shard_map/ppermute | solution.py:388
  134.2 5.4 %collective-permute-start.19 = (f32[2,8,128]{2,1,0:T(8,128)S(1)}, f32[2,8,128]{2,1,0:T(8,128)S(1)}, u32[]{:S(2)}, u32[]{:S(2)}) collective-permute-start(f32[2,8,128]{2,1,0:T(8,128)S(1)} %add_add_fusion.1.refs_2_), channel_id=1, source_target_pairs={{0,8},{4,12},{8,0},{12,4},{1,9},{5,13},{9,1},{13,5},{2,10},{6,14},... | collective-permute-start | bytes 24584 | tf_op jit(solution)/shard_map/ppermute | solution.py:388
  137.7 3.7 %collective-permute-start.20 = (f32[2,8,128]{2,1,0:T(8,128)S(1)}, f32[2,8,128]{2,1,0:T(8,128)S(1)}, u32[]{:S(2)}, u32[]{:S(2)}) collective-permute-start(f32[2,8,128]{2,1,0:T(8,128)S(1)} %add_add_fusion.1.refs_2_), channel_id=1, source_target_pairs={{0,12},{4,0},{8,4},{12,8},{1,13},{5,1},{9,5},{13,9},{2,14},{6,2},{... | collective-permute-start | bytes 24584 | tf_op jit(solution)/shard_map/ppermute | solution.py:388
  138.4 5.8 %copy-start = (bf16[4608,512]{1,0:T(8,128)(2,1)}, bf16[4608,512]{1,0:T(8,128)(2,1)S(1)}, u32[]{:S(2)}) copy-start(bf16[4608,512]{1,0:T(8,128)(2,1)S(1)} %constant_dynamic-update-slice_fusion.r_ref.refs_2_) | copy-start | bytes 14155780
  150.6 18.6 %collective-permute-start.21 = (bf16[256,1152]{1,0:T(8,128)(2,1)S(1)}, bf16[256,1152]{1,0:T(8,128)(2,1)S(1)}, u32[]{:S(2)}, u32[]{:S(2)}) collective-permute-start(bf16[256,1152]{1,0:T(8,128)(2,1)S(1)} %partial_pass.4.k_ref), channel_id=1, source_target_pairs={{0,4},{12,8},{1,5},{13,9},{2,6},{14,10},{3,7},{15,11},{16,20},{28,... | collective-permute-start | bytes 1769480 | tf_op jit(solution)/shard_map/ppermute | solution.py:445
  160.0 20.6 %collective-permute-start.22 = (bf16[256,1152]{1,0:T(8,128)(2,1)S(1)}, bf16[256,1152]{1,0:T(8,128)(2,1)S(1)}, u32[]{:S(2)}, u32[]{:S(2)}) collective-permute-start(bf16[256,1152]{1,0:T(8,128)(2,1)S(1)} %partial_pass.5.k_ref), channel_id=1, source_target_pairs={{0,4},{12,8},{1,5},{13,9},{2,6},{14,10},{3,7},{15,11},{16,20},{28,... | collective-permute-start | bytes 1769480 | tf_op jit(solution)/shard_map/ppermute | solution.py:445
  167.8 24.6 %collective-permute-start.24 = (bf16[256,1152]{1,0:T(8,128)(2,1)S(1)}, bf16[256,1152]{1,0:T(8,128)(2,1)S(1)}, u32[]{:S(2)}, u32[]{:S(2)}) collective-permute-start(bf16[256,1152]{1,0:T(8,128)(2,1)S(1)} %partial_pass.6), channel_id=1, source_target_pairs={{0,4},{12,8},{1,5},{13,9},{2,6},{14,10},{3,7},{15,11},{16,20},{28,... | collective-permute-start | bytes 1769480 | tf_op jit(solution)/shard_map/ppermute | solution.py:445
  169.3 12.2 %collective-permute-start.23 = (bf16[256,1152]{1,0:T(8,128)(2,1)S(1)}, bf16[256,1152]{1,0:T(8,128)(2,1)S(1)}, u32[]{:S(2)}, u32[]{:S(2)}) collective-permute-start(bf16[256,1152]{1,0:T(8,128)(2,1)S(1)} %add_convert_fusion.7.k_ref), channel_id=1, source_target_pairs={{4,8},{8,4},{5,9},{9,5},{6,10},{10,6},{7,11},{11,7},{20,24},{24,20... | collective-permute-start | bytes 1769480 | tf_op jit(solution)/shard_map/ppermute | solution.py:451
  176.4 25.5 %collective-permute-start.26 = (bf16[256,1152]{1,0:T(8,128)(2,1)S(1)}, bf16[256,1152]{1,0:T(8,128)(2,1)S(1)}, u32[]{:S(2)}, u32[]{:S(2)}) collective-permute-start(bf16[256,1152]{1,0:T(8,128)(2,1)S(1)} %partial_pass.7), channel_id=1, source_target_pairs={{0,4},{12,8},{1,5},{13,9},{2,6},{14,10},{3,7},{15,11},{16,20},{28,... | collective-permute-start | bytes 1769480 | tf_op jit(solution)/shard_map/ppermute | solution.py:445
  180.8 12.4 %collective-permute-start.25 = (bf16[256,1152]{1,0:T(8,128)(2,1)S(1)}, bf16[256,1152]{1,0:T(8,128)(2,1)S(1)}, u32[]{:S(2)}, u32[]{:S(2)}) collective-permute-start(bf16[256,1152]{1,0:T(8,128)(2,1)S(1)} %add_convert_fusion.6), channel_id=1, source_target_pairs={{4,8},{8,4},{5,9},{9,5},{6,10},{10,6},{7,11},{11,7},{20,24},{24,20... | collective-permute-start | bytes 1769480 | tf_op jit(solution)/shard_map/ppermute | solution.py:451
  181.7 21.1 %collective-permute-start.27 = (bf16[256,1152]{1,0:T(8,128)(2,1)S(1)}, bf16[256,1152]{1,0:T(8,128)(2,1)S(1)}, u32[]{:S(2)}, u32[]{:S(2)}) collective-permute-start(bf16[256,1152]{1,0:T(8,128)(2,1)S(1)} %add_convert_fusion.5.t_ref), channel_id=1, source_target_pairs={{4,0},{8,12},{5,1},{9,13},{6,2},{10,14},{7,3},{11,15},{20,16},{24,... | collective-permute-start | bytes 1769480 | tf_op jit(solution)/shard_map/ppermute | solution.py:457
  192.5 13.9 %collective-permute-start.28 = (bf16[256,1152]{1,0:T(8,128)(2,1)S(1)}, bf16[256,1152]{1,0:T(8,128)(2,1)S(1)}, u32[]{:S(2)}, u32[]{:S(2)}) collective-permute-start(bf16[256,1152]{1,0:T(8,128)(2,1)S(1)} %add_convert_fusion.4), channel_id=1, source_target_pairs={{4,8},{8,4},{5,9},{9,5},{6,10},{10,6},{7,11},{11,7},{20,24},{24,20... | collective-permute-start | bytes 1769480 | tf_op jit(solution)/shard_map/ppermute | solution.py:451
  193.4 15.0 %collective-permute-start.29 = (bf16[256,1152]{1,0:T(8,128)(2,1)S(1)}, bf16[256,1152]{1,0:T(8,128)(2,1)S(1)}, u32[]{:S(2)}, u32[]{:S(2)}) collective-permute-start(bf16[256,1152]{1,0:T(8,128)(2,1)S(1)} %add_convert_fusion.3.t_ref), channel_id=1, source_target_pairs={{4,0},{8,12},{5,1},{9,13},{6,2},{10,14},{7,3},{11,15},{20,16},{24,... | collective-permute-start | bytes 1769480 | tf_op jit(solution)/shard_map/ppermute | solution.py:457
  202.1 9.9 %collective-permute-start.30 = (bf16[256,1152]{1,0:T(8,128)(2,1)S(1)}, bf16[256,1152]{1,0:T(8,128)(2,1)S(1)}, u32[]{:S(2)}, u32[]{:S(2)}) collective-permute-start(bf16[256,1152]{1,0:T(8,128)(2,1)S(1)} %add_convert_fusion.2), channel_id=1, source_target_pairs={{4,8},{8,4},{5,9},{9,5},{6,10},{10,6},{7,11},{11,7},{20,24},{24,20... | collective-permute-start | bytes 1769480 | tf_op jit(solution)/shard_map/ppermute | solution.py:451
  206.5 17.3 %collective-permute-start.31 = (bf16[256,1152]{1,0:T(8,128)(2,1)S(1)}, bf16[256,1152]{1,0:T(8,128)(2,1)S(1)}, u32[]{:S(2)}, u32[]{:S(2)}) collective-permute-start(bf16[256,1152]{1,0:T(8,128)(2,1)S(1)} %add_convert_fusion.1.t_ref), channel_id=1, source_target_pairs={{4,0},{8,12},{5,1},{9,13},{6,2},{10,14},{7,3},{11,15},{20,16},{24,... | collective-permute-start | bytes 1769480 | tf_op jit(solution)/shard_map/ppermute | solution.py:457
  212.2 23.0 %collective-permute-start.32 = (bf16[256,1152]{1,0:T(8,128)(2,1)S(1)}, bf16[256,1152]{1,0:T(8,128)(2,1)S(1)}, u32[]{:S(2)}, u32[]{:S(2)}) collective-permute-start(bf16[256,1152]{1,0:T(8,128)(2,1)S(1)} %add_convert_fusion.t_ref), channel_id=1, source_target_pairs={{4,0},{8,12},{5,1},{9,13},{6,2},{10,14},{7,3},{11,15},{20,16},{24,... | collective-permute-start | bytes 1769480 | tf_op jit(solution)/shard_map/ppermute | solution.py:457
  238.8 3.1 %collective-permute-start.34 = (f32[2,8,128]{2,1,0:T(8,128)S(1)}, f32[2,8,128]{2,1,0:T(8,128)S(1)}, u32[]{:S(2)}, u32[]{:S(2)}) collective-permute-start(f32[2,8,128]{2,1,0:T(8,128)S(1)} %get-tuple-element.82), channel_id=1, source_target_pairs={{0,1},{1,2},{2,3},{3,0},{4,5},{5,6},{6,7},{7,4},{8,9},{9,10},{10,1... | collective-permute-start | bytes 24584 | tf_op jit(solution)/shard_map/ppermute | solution.py:388
  238.9 3.1 %collective-permute-start.35 = (f32[2,8,128]{2,1,0:T(8,128)S(1)}, f32[2,8,128]{2,1,0:T(8,128)S(1)}, u32[]{:S(2)}, u32[]{:S(2)}) collective-permute-start(f32[2,8,128]{2,1,0:T(8,128)S(1)} %get-tuple-element.82), channel_id=1, source_target_pairs={{0,3},{1,0},{2,1},{3,2},{4,7},{5,4},{6,5},{7,6},{8,11},{9,8},{10,9... | collective-permute-start | bytes 24584 | tf_op jit(solution)/shard_map/ppermute | solution.py:388
  240.6 3.7 %collective-permute-start.33 = (f32[2,8,128]{2,1,0:T(8,128)S(1)}, f32[2,8,128]{2,1,0:T(8,128)S(1)}, u32[]{:S(2)}, u32[]{:S(2)}) collective-permute-start(f32[2,8,128]{2,1,0:T(8,128)S(1)} %get-tuple-element.82), channel_id=1, source_target_pairs={{0,2},{1,3},{2,0},{3,1},{4,6},{5,7},{6,4},{7,5},{8,10},{9,11},{10,... | collective-permute-start | bytes 24584 | tf_op jit(solution)/shard_map/ppermute | solution.py:388
  244.3 5.4 %collective-permute-start.36 = (f32[2,8,128]{2,1,0:T(8,128)S(1)}, f32[2,8,128]{2,1,0:T(8,128)S(1)}, u32[]{:S(2)}, u32[]{:S(2)}) collective-permute-start(f32[2,8,128]{2,1,0:T(8,128)S(1)} %add_add_fusion.refs_8_), channel_id=1, source_target_pairs={{0,4},{4,8},{8,12},{12,0},{1,5},{5,9},{9,13},{13,1},{2,6},{6,10},{... | collective-permute-start | bytes 24584 | tf_op jit(solution)/shard_map/ppermute | solution.py:388
  244.3 5.4 %collective-permute-start.37 = (f32[2,8,128]{2,1,0:T(8,128)S(1)}, f32[2,8,128]{2,1,0:T(8,128)S(1)}, u32[]{:S(2)}, u32[]{:S(2)}) collective-permute-start(f32[2,8,128]{2,1,0:T(8,128)S(1)} %add_add_fusion.refs_8_), channel_id=1, source_target_pairs={{0,8},{4,12},{8,0},{12,4},{1,9},{5,13},{9,1},{13,5},{2,10},{6,14},... | collective-permute-start | bytes 24584 | tf_op jit(solution)/shard_map/ppermute | solution.py:388
  246.9 3.7 %collective-permute-start.38 = (f32[2,8,128]{2,1,0:T(8,128)S(1)}, f32[2,8,128]{2,1,0:T(8,128)S(1)}, u32[]{:S(2)}, u32[]{:S(2)}) collective-permute-start(f32[2,8,128]{2,1,0:T(8,128)S(1)} %add_add_fusion.refs_8_), channel_id=1, source_target_pairs={{0,12},{4,0},{8,4},{12,8},{1,13},{5,1},{9,5},{13,9},{2,14},{6,2},{... | collective-permute-start | bytes 24584 | tf_op jit(solution)/shard_map/ppermute | solution.py:388
where the time goes:
time: 271 us; the launch traced here: 270 us
  waiting for transfers between devices  114 us (42%)
  Pallas kernels  100 us (37%)
  starting transfers between devices  46.1 us (17%)
  local copies, waits for them, and re-layouts  5.56 us (2%)
  other arithmetic  2.97 us (1%)
    pallas_call x3, Pallas kernels, first_pass(): pl.pallas_call(functools.partial(first_kernel, tuple((len(g) for g in gro...  29.5 us
    pallas_call x4, Pallas kernels, partial_pass(): pl.pallas_call(functools.partial(partial_kernel, tile), grid=(width // bn...  25.7 us
    ppermute x1, waiting for transfers between devices, body(): outer = lax.ppermute(out_grads, 'row', outward)  23.9 us
    pallas_call x1, Pallas kernels, last_pass(): pl.pallas_call(functools.partial(last_kernel, pick(m, TILE), copies, tupl...  19.5 us
    ppermute x4, waiting for transfers between devices, back(): backs[k] = lax.ppermute(totals[k], axis, [(1, 0), (2, 3)])  18.7 us
    ppermute x4, waiting for transfers between devices, half(): came = lax.ppermute(sent[k], axis, [(0, 1), (3, 2)])  16.6 us
    ppermute x1, waiting for transfers between devices, body(): early = lax.ppermute(inners[0], 'row', onward)  14.4 us
    pallas_call x4, Pallas kernels, right_curve(): pl.pallas_call(functools.partial(right_curve_kernel, pick(m, TILE)), grid...  14.3 us
  transfers between devices with their start and end apart: 39, of which 19 were waited for; matrix products, arithmetic and copies ran while one was open for 2% of the time, Pallas kernels for 20%

commit v1 on v0

--- a/solution.py
+++ b/solution.py
@@ -178,7 +178,7 @@
 def left_curve(side, halves, right, f):
     m, n = f.shape
     rank = right.shape[1]
-    bn = pick(n, 2 * BLOCK)
+    bn = pick(n, 3 * BLOCK)
     half = pl.BlockSpec((m // 2, rank), lambda j: (0, 0))
     return pl.pallas_call(
         functools.partial(left_curve_kernel, pick(m, TILE)),
@@ -229,7 +229,7 @@
         compiler_params=pltpu.CompilerParams(vmem_limit_bytes=LIMIT),
         cost_estimate=pl.CostEstimate(flops=2 * m * width * rank, bytes_accessed=2 * m * width, transcendentals=0),
         name="right_curve",
-    )(flag, far(left_new), total, back, far(f), sums)
+    )(flag, left_new, total, back, far(f), sums)
 
 
 def left_new_kernel(copies, *refs):
@@ -253,12 +253,12 @@
     m, rank = left.shape
     return pl.pallas_call(
         functools.partial(left_new_kernel, copies),
-        out_shape=[jax.ShapeDtypeStruct((8, 128), f32), pltpu.HBM((m, rank), bf16), pltpu.VMEM((rank, m), bf16),
+        out_shape=[jax.ShapeDtypeStruct((8, 128), f32), pltpu.VMEM((m, rank), bf16), pltpu.VMEM((rank, m), bf16),
                    pltpu.VMEM((m, 2 * rank), bf16)],
         compiler_params=pltpu.CompilerParams(vmem_limit_bytes=LIMIT),
         cost_estimate=pl.CostEstimate(flops=2 * m * rank, bytes_accessed=10 * m * rank, transcendentals=0),
         name="left_update",
-    )(far(left), near(descent), *pieces)
+    )(left, near(descent), *pieces)
 
 
 def partial_kernel(tile, p_ref, w_ref, r_ref, f_ref, t_ref, k_ref, o_ref, acc_ref):
@@ -352,7 +352,7 @@
         compiler_params=pltpu.CompilerParams(vmem_limit_bytes=LIMIT),
         cost_estimate=pl.CostEstimate(flops=6 * m * n * rank, bytes_accessed=4 * m * n, transcendentals=0),
         name="last_pass",
-    )(far(w), near(pair), far(twice), far(left_new), *parts, *pieces)
+    )(far(w), near(pair), far(twice), left_new, *parts, *pieces)
 
 
 FIRST = (3, 2, 1)
@@ -500,7 +500,7 @@
                 ends = [(end, shard, 0, False), (end, shard, 1, False)]
             groups = [[(out_grads, shard, 0, True)], [(outer, shard, 0, True)],
                       [(inner, shard, 0, True), ends[0]], [(crossed[k], shard, 0, False), ends[1]]]
-            prev = first_pass(at, matrix, left, right, groups, offset, width, prev, BLOCK, TILE)
+            prev = first_pass(at, matrix, left, right, groups, offset, width, prev, BLOCK, 2 * TILE)
             partials.append(prev[1])
     else:
         gathered = lax.all_gather(activations, "col", axis=0, tiled=True)

time: 271 us -> 269 us (level)
  Pallas kernels: 100 us -> 96.2 us
  transfers between devices with their start and end apart: 39 -> 39, of which waited for: 19 -> 18; matrix products, arithmetic and copies ran while one was open for 2% -> 3% of each run, Pallas kernels for 20% -> 19%
where the time goes in v1:
time: 269 us; the launch traced here: 268 us
  waiting for transfers between devices  112 us (42%)
  Pallas kernels  96.2 us (36%)
  starting transfers between devices  47.7 us (18%)
  local copies, waits for them, and re-layouts  6.44 us (2%)
  other arithmetic  4.22 us (2%)
    pallas_call x3, Pallas kernels, first_pass(): pl.pallas_call(functools.partial(first_kernel, tuple((len(g) for g in gro...  28.4 us
    pallas_call x4, Pallas kernels, partial_pass(): pl.pallas_call(functools.partial(partial_kernel, tile), grid=(width // bn...  26.4 us
    ppermute x1, waiting for transfers between devices, body(): outer = lax.ppermute(out_grads, 'row', outward)  23.9 us
    ppermute x4, waiting for transfers between devices, back(): backs[k] = lax.ppermute(totals[k], axis, [(1, 0), (2, 3)])  19.3 us
    pallas_call x1, Pallas kernels, last_pass(): pl.pallas_call(functools.partial(last_kernel, pick(m, TILE), copies, tupl...  19.3 us
    ppermute x4, waiting for transfers between devices, half(): came = lax.ppermute(sent[k], axis, [(0, 1), (3, 2)])  15.6 us
    ppermute x1, waiting for transfers between devices, body(): early = lax.ppermute(inners[0], 'row', onward)  14.4 us
    ppermute x12, starting transfers between devices, pieces_of(): return [x] + [lax.ppermute(x, axis, turned(4, k)) for k in (1, 2, 3)]  14.1 us
  transfers between devices with their start and end apart: 39, of which 18 were waited for; matrix products, arithmetic and copies ran while one was open for 3% of the time, Pallas kernels for 19%

profile of v1, /device:TPU:0, one launch (start us, length us, event | category | flops | bytes accessed | tf_op | source)
XLA Modules:
  0.0 267.7 jit_solution(18206978605611676241)
XLA Ops:
  0.6 3.1 %collective-permute-start.2 = (bf16[128,4608]{1,0:T(8,128)(2,1)}, bf16[128,4608]{1,0:T(8,128)(2,1)S(1)}, u32[]{:S(2)}, u32[]{:S(2)}) collective-permute-start(bf16[128,4608]{1,0:T(8,128)(2,1)} %refs_4_.5), channel_id=1, source_target_pairs={{0,4},{4,0},{8,12},{12,8},{1,5},{5,1},{9,13},{13,9},{2,6},{6,2},{1... | collective-permute-start | bytes 3538952 | tf_op jit(solution)/shard_map/ppermute | solution.py:476
  3.7 0.7 collective-permute-start.5
  4.5 1.6 collective-permute-start.1
  6.0 23.9 %collective-permute-done.2.refs_5_ = bf16[128,4608]{1,0:T(8,128)(2,1)S(1)} collective-permute-done((bf16[128,4608]{1,0:T(8,128)(2,1)}, bf16[128,4608]{1,0:T(8,128)(2,1)S(1)}, u32[]{:S(2)}, u32[]{:S(2)}) %collective-permute-start.2) | collective-permute-done | bytes 1179680 | tf_op jit(solution)/shard_map/ppermute | solution.py:476
  30.0 1.6 collective-permute-start.3
  31.7 1.3 collective-permute-start.7
  33.1 0.8 slice.29
  34.6 14.4 %collective-permute-done.7.refs_7_ = bf16[128,2304]{1,0:T(8,128)(2,1)} collective-permute-done((bf16[128,2304]{1,0:T(8,128)(2,1)S(1)}, bf16[128,2304]{1,0:T(8,128)(2,1)}, u32[]{:S(2)}, u32[]{:S(2)}) %collective-permute-start.7) | collective-permute-done | bytes 589856 | tf_op jit(solution)/shard_map/ppermute | solution.py:493
  49.0 1.3 collective-permute-start.8
  51.0 1.3 pad_maximum_fusion
  53.6 0.8 slice-done.1
  54.4 1.3 collective-permute-start.11
  55.8 11.8 %collective-permute-done.8.refs_9_ = bf16[128,2304]{1,0:T(8,128)(2,1)S(1)} collective-permute-done((bf16[128,2304]{1,0:T(8,128)(2,1)}, bf16[128,2304]{1,0:T(8,128)(2,1)S(1)}, u32[]{:S(2)}, u32[]{:S(2)}) %collective-permute-start.8) | collective-permute-done | bytes 589856 | tf_op jit(solution)/shard_map/ppermute | solution.py:494
  67.6 0.8 copy-done.12
  68.4 12.3 %first_pass.3 = (bf16[1536,4608]{1,0:T(8,128)(2,1)}, f32[1536,256]{1,0:T(8,128)S(1)}) custom-call(bf16[1536,512]{1,0:T(8,128)(2,1)S(1)} %maximum_bitcast_fusion.refs_0_, bf16[1536,4608]{1,0:T(8,128)(2,1)} %refs_0_.3, bf16[1536,256]{1,0:T(8,128)(2,1)} %refs_0_.2, bf16[4608,256]{1,0:T(8,128)(2,1)} %r_ref.1, bf16[128,4608]{1,0:T(8,128)(2,1)} %refs_4_.5, ...), custom_call_target="tpu_custom_call" | custom-call | flops 7247757312 | bytes 14155776 | tf_op jit(solution)/shard_map/first_pass/pallas_call | solution.py:129
  80.6 1.5 collective-permute-start.9
  82.1 3.9 %collective-permute-done.11.refs_7_.refs_9_ = bf16[256,1536]{1,0:T(8,128)(2,1)S(1)} collective-permute-done((bf16[256,1536]{1,0:T(8,128)(2,1)S(1)}, bf16[256,1536]{1,0:T(8,128)(2,1)S(1)}, u32[]{:S(2)}, u32[]{:S(2)}) %collective-permute-start.11) | collective-permute-done | bytes 786464 | tf_op jit(solution)/shard_map/ppermute | solution.py:499
  86.0 0.9 copy-done.5
  86.9 10.2 %first_pass.4 = (bf16[1536,4608]{1,0:T(8,128)(2,1)}, f32[1536,256]{1,0:T(8,128)S(1)}) custom-call(bf16[1536,512]{1,0:T(8,128)(2,1)S(1)} %maximum_bitcast_fusion.refs_0_, bf16[1536,4608]{1,0:T(8,128)(2,1)} %refs_0_.3, bf16[1536,256]{1,0:T(8,128)(2,1)} %refs_0_.2, bf16[4608,256]{1,0:T(8,128)(2,1)} %r_ref.1, ...), custom_call_target="tpu_custom_call", output_to_operand_aliasing={{1}: (10, {}), {0}: (11, {})} | custom-call | flops 4831838208 | bytes 9437184 | tf_op jit(solution)/shard_map/first_pass/pallas_call | solution.py:129
  97.1 0.7 copy-done.6
  97.8 6.0 %first_pass.5 = (bf16[1536,4608]{1,0:T(8,128)(2,1)}, f32[1536,256]{1,0:T(8,128)S(1)}) custom-call(bf16[1536,512]{1,0:T(8,128)(2,1)S(1)} %maximum_bitcast_fusion.refs_0_, bf16[1536,4608]{1,0:T(8,128)(2,1)} %refs_0_.3, bf16[1536,256]{1,0:T(8,128)(2,1)} %refs_0_.2, bf16[4608,256]{1,0:T(8,128)(2,1)} %r_ref.1, ...), custom_call_target="tpu_custom_call", output_to_operand_aliasing={{1}: (10, {}), {0}: (11, {})} | custom-call | flops 2415919104 | bytes 4718592 | tf_op jit(solution)/shard_map/first_pass/pallas_call | solution.py:129
  104.0 2.3 collective-permute-done.12
  106.4 1.6 collective-permute-start.13
  107.9 9.7 %collective-permute-done.13 = bf16[768,256]{1,0:T(8,128)(2,1)S(1)} collective-permute-done((bf16[768,256]{1,0:T(8,128)(2,1)S(1)}, bf16[768,256]{1,0:T(8,128)(2,1)S(1)}, u32[]{:S(2)}, u32[]{:S(2)}) %collective-permute-start.13) | collective-permute-done | bytes 393248 | tf_op jit(solution)/shard_map/ppermute | solution.py:422
  117.8 2.3 collective-permute-done.14.c_ref
  120.0 8.0 %left_curve.1 = (f32[2,8,128]{2,1,0:T(8,128)S(1)}, f32[1536,256]{1,0:T(8,128)S(1)}) custom-call(s32[1,1]{1,0:T(1,128)} %bitcast.side_ref, f32[768,256]{1,0:T(8,128)S(1)} %convert_add_fusion.b_ref, f32[768,256]{1,0:T(8,128)S(1)} %collective-permute-done.14.c_ref, bf16[4608,256]{1,0:T(8,128)(2,1)} %r_ref.1, bf16[1536,4608]{1,0:T(8,128)(2,1)} %get-tuple-element.56.f_ref), custom_call_target="tpu_custom_call" | custom-call | flops 3623878656 | bytes 14155776 | tf_op jit(solution)/shard_map/left_curve/pallas_call | solution.py:183
  128.2 1.6 collective-permute-start.17
  129.8 1.5 collective-permute-start.15
  131.5 1.9 collective-permute-done.15
  133.5 3.3 %collective-permute-start.19 = (f32[2,8,128]{2,1,0:T(8,128)S(1)}, f32[2,8,128]{2,1,0:T(8,128)S(1)}, u32[]{:S(2)}, u32[]{:S(2)}) collective-permute-start(f32[2,8,128]{2,1,0:T(8,128)S(1)} %add_add_fusion.1.refs_2_), channel_id=1, source_target_pairs={{0,8},{4,12},{8,0},{12,4},{1,9},{5,13},{9,1},{13,5},{2,10},{6,14},... | collective-permute-start | bytes 24584 | tf_op jit(solution)/shard_map/ppermute | solution.py:388
  137.5 1.4 collective-permute-done.18.refs_3_
  138.9 1.5 collective-permute-done.20.refs_5_
  140.4 0.8 left_update.1
  141.2 7.1 %partial_pass.4.k_ref = bf16[256,1152]{1,0:T(8,128)(2,1)} custom-call(bf16[1536,512]{1,0:T(8,128)(2,1)S(1)} %get-tuple-element.60.p_ref.refs_1_, bf16[1536,4608]{1,0:T(8,128)(2,1)} %refs_0_.3, bf16[4608,512]{1,0:T(8,128)(2,1)} %copy-done.1, bf16[1536,4608]{1,0:T(8,128)(2,1)} %get-tuple-element.56.f_ref, bf16[256,1536]{1,0:T(8,128)(2,1)S(1)} %get-tuple-element.61.t_ref, ...), custom_call_target="tpu_custom_call" | custom-call | flops 2717908992 | bytes 7077888 | tf_op jit(solution)/shard_map/partial_pass/pallas_call | solution.py:285
  148.3 3.9 %collective-permute-start.21 = (bf16[256,1152]{1,0:T(8,128)(2,1)}, bf16[256,1152]{1,0:T(8,128)(2,1)}, u32[]{:S(2)}, u32[]{:S(2)}) collective-permute-start(bf16[256,1152]{1,0:T(8,128)(2,1)} %partial_pass.4.k_ref), channel_id=1, source_target_pairs={{0,4},{12,8},{1,5},{13,9},{2,6},{14,10},{3,7},{15,11},{16,20},{28,... | collective-permute-start | bytes 1769480 | tf_op jit(solution)/shard_map/ppermute | solution.py:445
  152.2 6.4 %partial_pass.5.k_ref = bf16[256,1152]{1,0:T(8,128)(2,1)S(1)} custom-call(bf16[1536,512]{1,0:T(8,128)(2,1)S(1)} %get-tuple-element.60.p_ref.refs_1_, bf16[1536,4608]{1,0:T(8,128)(2,1)} %refs_0_.3, bf16[4608,512]{1,0:T(8,128)(2,1)} %copy-done.1, bf16[1536,4608]{1,0:T(8,128)(2,1)} %get-tuple-element.56.f_ref, bf16[256,1536]{1,0:T(8,128)(2,1)S(1)} %get-tuple-element.61.t_ref, ...), custom_call_target="tpu_custom_call" | custom-call | flops 2717908992 | bytes 7077888 | tf_op jit(solution)/shard_map/partial_pass/pallas_call | solution.py:285
  158.6 1.3 collective-permute-start.22
  159.9 6.4 %partial_pass.6 = bf16[256,1152]{1,0:T(8,128)(2,1)S(1)} custom-call(bf16[1536,512]{1,0:T(8,128)(2,1)S(1)} %get-tuple-element.60.p_ref.refs_1_, bf16[1536,4608]{1,0:T(8,128)(2,1)} %refs_0_.3, bf16[4608,512]{1,0:T(8,128)(2,1)} %copy-done.1, bf16[1536,4608]{1,0:T(8,128)(2,1)} %get-tuple-element.56.f_ref, bf16[256,1536]{1,0:T(8,128)(2,1)S(1)} %get-tuple-element.61.t_ref, ...), custom_call_target="tpu_custom_call" | custom-call | flops 2717908992 | bytes 7077888 | tf_op jit(solution)/shard_map/partial_pass/pallas_call | solution.py:285
  166.4 1.3 collective-permute-start.24
  167.7 1.4 add_convert_fusion.7.k_ref
  169.8 6.4 %partial_pass.7 = bf16[256,1152]{1,0:T(8,128)(2,1)S(1)} custom-call(bf16[1536,512]{1,0:T(8,128)(2,1)S(1)} %get-tuple-element.60.p_ref.refs_1_, bf16[1536,4608]{1,0:T(8,128)(2,1)} %refs_0_.3, bf16[4608,512]{1,0:T(8,128)(2,1)} %copy-done.1, bf16[1536,4608]{1,0:T(8,128)(2,1)} %get-tuple-element.56.f_ref, bf16[256,1536]{1,0:T(8,128)(2,1)S(1)} %get-tuple-element.61.t_ref, ...), custom_call_target="tpu_custom_call" | custom-call | flops 2717908992 | bytes 7077888 | tf_op jit(solution)/shard_map/partial_pass/pallas_call | solution.py:285
  176.3 3.7 %collective-permute-start.26 = (bf16[256,1152]{1,0:T(8,128)(2,1)S(1)}, bf16[256,1152]{1,0:T(8,128)(2,1)S(1)}, u32[]{:S(2)}, u32[]{:S(2)}) collective-permute-start(bf16[256,1152]{1,0:T(8,128)(2,1)S(1)} %partial_pass.7), channel_id=1, source_target_pairs={{0,4},{12,8},{1,5},{13,9},{2,6},{14,10},{3,7},{15,11},{16,20},{28,... | collective-permute-start | bytes 1769480 | tf_op jit(solution)/shard_map/ppermute | solution.py:445
  181.0 1.3 collective-permute-start.27
  182.3 8.3 %collective-permute-done.24 = bf16[256,1152]{1,0:T(8,128)(2,1)S(1)} collective-permute-done((bf16[256,1152]{1,0:T(8,128)(2,1)S(1)}, bf16[256,1152]{1,0:T(8,128)(2,1)S(1)}, u32[]{:S(2)}, u32[]{:S(2)}) %collective-permute-start.24) | collective-permute-done | bytes 589856 | tf_op jit(solution)/shard_map/ppermute | solution.py:445
  191.6 1.3 collective-permute-start.29
  192.9 7.2 %collective-permute-done.26 = bf16[256,1152]{1,0:T(8,128)(2,1)S(1)} collective-permute-done((bf16[256,1152]{1,0:T(8,128)(2,1)S(1)}, bf16[256,1152]{1,0:T(8,128)(2,1)S(1)}, u32[]{:S(2)}, u32[]{:S(2)}) %collective-permute-start.26) | collective-permute-done | bytes 589856 | tf_op jit(solution)/shard_map/ppermute | solution.py:445
  201.1 3.3 %right_curve.4 = (f32[2,8,128]{2,1,0:T(8,128)S(1)}, bf16[256,1152]{1,0:T(8,128)(2,1)S(1)}) custom-call(s32[1,1]{1,0:T(1,128)} %bitcast.10.flag_ref, bf16[1536,256]{1,0:T(8,128)(2,1)S(1)} %get-tuple-element.89.a_ref.refs_3_, bf16[256,1152]{1,0:T(8,128)(2,1)S(1)} %add_convert_fusion.5.t_ref, bf16[256,1152]{1,0:T(8,128)(2,1)S(1)} %collective-permute-done.27.b_ref, ...), custom_call_target="tpu_custom_call" | custom-call | flops 905969664 | bytes 3538944 | tf_op jit(solution)/shard_map/right_curve/pallas_call | solution.py:222
  204.6 1.3 collective-permute-start.31
  205.9 2.5 collective-permute-done.29.b_ref
  208.3 3.3 %right_curve.5 = (f32[2,8,128]{2,1,0:T(8,128)S(1)}, bf16[256,1152]{1,0:T(8,128)(2,1)S(1)}) custom-call(s32[1,1]{1,0:T(1,128)} %bitcast.10.flag_ref, bf16[1536,256]{1,0:T(8,128)(2,1)S(1)} %get-tuple-element.89.a_ref.refs_3_, bf16[256,1152]{1,0:T(8,128)(2,1)S(1)} %add_convert_fusion.3.t_ref, bf16[256,1152]{1,0:T(8,128)(2,1)S(1)} %collective-permute-done.29.b_ref, ...), custom_call_target="tpu_custom_call" | custom-call | flops 905969664 | bytes 3538944 | tf_op jit(solution)/shard_map/right_curve/pallas_call | solution.py:222
  211.8 1.3 collective-permute-start.32
  213.1 8.1 %collective-permute-done.31.b_ref = bf16[256,1152]{1,0:T(8,128)(2,1)S(1)} collective-permute-done((bf16[256,1152]{1,0:T(8,128)(2,1)S(1)}, bf16[256,1152]{1,0:T(8,128)(2,1)S(1)}, u32[]{:S(2)}, u32[]{:S(2)}) %collective-permute-start.31) | collective-permute-done | bytes 589856 | tf_op jit(solution)/shard_map/ppermute | solution.py:457
  221.3 3.3 %right_curve.6 = (f32[2,8,128]{2,1,0:T(8,128)S(1)}, bf16[256,1152]{1,0:T(8,128)(2,1)S(1)}) custom-call(s32[1,1]{1,0:T(1,128)} %bitcast.10.flag_ref, bf16[1536,256]{1,0:T(8,128)(2,1)S(1)} %get-tuple-element.89.a_ref.refs_3_, bf16[256,1152]{1,0:T(8,128)(2,1)S(1)} %add_convert_fusion.1.t_ref, bf16[256,1152]{1,0:T(8,128)(2,1)S(1)} %collective-permute-done.31.b_ref, ...), custom_call_target="tpu_custom_call" | custom-call | flops 905969664 | bytes 3538944 | tf_op jit(solution)/shard_map/right_curve/pallas_call | solution.py:222
  224.6 8.7 %collective-permute-done.32.b_ref = bf16[256,1152]{1,0:T(8,128)(2,1)S(1)} collective-permute-done((bf16[256,1152]{1,0:T(8,128)(2,1)S(1)}, bf16[256,1152]{1,0:T(8,128)(2,1)S(1)}, u32[]{:S(2)}, u32[]{:S(2)}) %collective-permute-start.32) | collective-permute-done | bytes 589856 | tf_op jit(solution)/shard_map/ppermute | solution.py:457
  233.3 3.3 %right_curve.7 = (f32[2,8,128]{2,1,0:T(8,128)S(1)}, bf16[256,1152]{1,0:T(8,128)(2,1)S(1)}) custom-call(s32[1,1]{1,0:T(1,128)} %bitcast.10.flag_ref, bf16[1536,256]{1,0:T(8,128)(2,1)S(1)} %get-tuple-element.89.a_ref.refs_3_, bf16[256,1152]{1,0:T(8,128)(2,1)S(1)} %add_convert_fusion.t_ref, bf16[256,1152]{1,0:T(8,128)(2,1)S(1)} %collective-permute-done.32.b_ref, ...), custom_call_target="tpu_custom_call" | custom-call | flops 905969664 | bytes 3538944 | tf_op jit(solution)/shard_map/right_curve/pallas_call | solution.py:222
  236.8 1.7 collective-permute-start.35
  238.5 1.4 collective-permute-start.33
  239.9 2.2 collective-permute-done.33
  242.2 2.5 collective-permute-start.37
  244.7 1.3 collective-permute-start.38
  246.0 0.9 copy.21
  246.9 0.7 collective-permute-done.36.refs_9_
  247.6 0.7 collective-permute-done.38.refs_11_
  248.3 19.3 %last_pass.1 = (bf16[1536,4608]{1,0:T(8,128)(2,1)}, bf16[4608,256]{1,0:T(8,128)(2,1)}) custom-call(bf16[1536,4608]{1,0:T(8,128)(2,1)} %refs_0_.3, bf16[1536,512]{1,0:T(8,128)(2,1)S(1)} %get-tuple-element.60.p_ref.refs_1_, bf16[4608,512]{1,0:T(8,128)(2,1)} %copy-done.1, bf16[1536,256]{1,0:T(8,128)(2,1)S(1)} %get-tuple-element.89.a_ref.refs_3_, ...), custom_call_target="tpu_custom_call" | custom-call | flops 10871635968 | bytes 28311552 | tf_op jit(solution)/shard_map/last_pass/pallas_call | solution.py:343
  (88 shorter events, 8.3 us)
Async XLA Ops:
  0.6 29.3 %collective-permute-start.2 = (bf16[128,4608]{1,0:T(8,128)(2,1)}, bf16[128,4608]{1,0:T(8,128)(2,1)S(1)}, u32[]{:S(2)}, u32[]{:S(2)}) collective-permute-start(bf16[128,4608]{1,0:T(8,128)(2,1)} %refs_4_.5), channel_id=1, source_target_pairs={{0,4},{4,0},{8,12},{12,8},{1,5},{5,1},{9,13},{13,9},{2,6},{6,2},{1... | collective-permute-start | bytes 3538952 | tf_op jit(solution)/shard_map/ppermute | solution.py:476
  3.7 27.9 %collective-permute-start.5 = (bf16[128,4608]{1,0:T(8,128)(2,1)}, bf16[128,4608]{1,0:T(8,128)(2,1)S(1)}, u32[]{:S(2)}, u32[]{:S(2)}) collective-permute-start(bf16[128,4608]{1,0:T(8,128)(2,1)} %refs_4_.5), channel_id=1, source_target_pairs={{4,8},{8,4},{5,9},{9,5},{6,10},{10,6},{7,11},{11,7},{20,24},{24,20... | collective-permute-start | bytes 3538952 | tf_op jit(solution)/shard_map/ppermute | solution.py:477
  4.5 25.5 %collective-permute-start.1 = (bf16[128,1536]{1,0:T(8,128)(2,1)}, bf16[128,1536]{1,0:T(8,128)(2,1)}, u32[]{:S(2)}, u32[]{:S(2)}) collective-permute-start(bf16[128,1536]{1,0:T(8,128)(2,1)} %param.5), channel_id=1, source_target_pairs={{0,2},{1,3},{2,0},{3,1},{4,6},{5,7},{6,4},{7,5},{8,10},{9,11},{10,... | collective-permute-start | bytes 1179656 | tf_op jit(solution)/shard_map/ppermute | solution.py:482
  6.0 24.0 %collective-permute-start = (bf16[128,1536]{1,0:T(8,128)(2,1)}, bf16[128,1536]{1,0:T(8,128)(2,1)S(1)}, u32[]{:S(2)}, u32[]{:S(2)}) collective-permute-start(bf16[128,1536]{1,0:T(8,128)(2,1)} %param.5), channel_id=1, source_target_pairs={{0,1},{1,0},{2,3},{3,2},{4,5},{5,4},{6,7},{7,6},{8,9},{9,8},{10,11... | collective-permute-start | bytes 1179656 | tf_op jit(solution)/shard_map/ppermute | solution.py:481
  29.9 3.2 %copy-start.3 = (bf16[128,4608]{1,0:T(8,128)(2,1)}, bf16[128,4608]{1,0:T(8,128)(2,1)S(1)}, u32[]{:S(2)}) copy-start(bf16[128,4608]{1,0:T(8,128)(2,1)S(1)} %collective-permute-done.2.refs_5_) | copy-start | bytes 3538948
  29.9 21.0 %copy-start.9 = (bf16[128,1536]{1,0:T(8,128)(2,1)S(1)}, bf16[128,1536]{1,0:T(8,128)(2,1)}, u32[]{:S(2)}) copy-start(bf16[128,1536]{1,0:T(8,128)(2,1)} %param.5) | copy-start | bytes 1179652
  30.0 3.0 %copy-start.10 = (bf16[128,1536]{1,0:T(8,128)(2,1)}, bf16[128,1536]{1,0:T(8,128)(2,1)S(1)}, u32[]{:S(2)}) copy-start(bf16[128,1536]{1,0:T(8,128)(2,1)S(1)} %collective-permute-done) | copy-start | bytes 1179652
  30.0 3.0 %collective-permute-start.3 = (bf16[128,2304]{1,0:T(8,128)(2,1)S(1)}, bf16[128,2304]{1,0:T(8,128)(2,1)}, u32[]{:S(2)}, u32[]{:S(2)}) collective-permute-start(bf16[128,2304]{1,0:T(8,128)(2,1)S(1)} %slice.24), channel_id=1, source_target_pairs={{4,8},{8,4},{5,9},{9,5},{6,10},{10,6},{7,11},{11,7},{20,24},{24,20... | collective-permute-start | bytes 1769480 | tf_op jit(solution)/shard_map/ppermute | solution.py:483
  31.6 2.3 copy-start.4
  31.7 17.3 %collective-permute-start.7 = (bf16[128,2304]{1,0:T(8,128)(2,1)S(1)}, bf16[128,2304]{1,0:T(8,128)(2,1)}, u32[]{:S(2)}, u32[]{:S(2)}) collective-permute-start(bf16[128,2304]{1,0:T(8,128)(2,1)S(1)} %slice.27), channel_id=1, source_target_pairs={{4,0},{8,12},{5,1},{9,13},{6,2},{10,14},{7,3},{11,15},{20,16},{24,... | collective-permute-start | bytes 1769480 | tf_op jit(solution)/shard_map/ppermute | solution.py:493
  33.0 18.0 %collective-permute-start.4 = (bf16[128,1536]{1,0:T(8,128)(2,1)}, bf16[128,1536]{1,0:T(8,128)(2,1)}, u32[]{:S(2)}, u32[]{:S(2)}) collective-permute-start(bf16[128,1536]{1,0:T(8,128)(2,1)} %collective-permute-done.1), channel_id=1, source_target_pairs={{0,1},{1,0},{2,3},{3,2},{4,5},{5,4},{6,7},{7,6},{8,9},{9,8},{10,11... | collective-permute-start | bytes 1179656 | tf_op jit(solution)/shard_map/ppermute | solution.py:485
  33.1 17.9 %copy-start.11 = (bf16[128,1536]{1,0:T(8,128)(2,1)S(1)}, bf16[128,1536]{1,0:T(8,128)(2,1)}, u32[]{:S(2)}) copy-start(bf16[128,1536]{1,0:T(8,128)(2,1)} %copy-done.10) | copy-start | bytes 1179652
  33.9 21.8 %collective-permute-start.6 = (bf16[128,768]{1,0:T(8,128)(2,1)S(1)}, bf16[128,768]{1,0:T(8,128)(2,1)S(1)}, u32[]{:S(2)}, u32[]{:S(2)}) collective-permute-start(bf16[128,768]{1,0:T(8,128)(2,1)S(1)} %slice.26), channel_id=1, source_target_pairs={{4,8},{8,4},{5,9},{9,5},{6,10},{10,6},{7,11},{11,7},{20,24},{24,20... | collective-permute-start | bytes 589832 | tf_op jit(solution)/shard_map/ppermute | solution.py:484
  49.0 18.6 %collective-permute-start.8 = (bf16[128,2304]{1,0:T(8,128)(2,1)}, bf16[128,2304]{1,0:T(8,128)(2,1)S(1)}, u32[]{:S(2)}, u32[]{:S(2)}) collective-permute-start(bf16[128,2304]{1,0:T(8,128)(2,1)} %collective-permute-done.3.refs_8_), channel_id=1, source_target_pairs={{4,0},{8,12},{5,1},{9,13},{6,2},{10,14},{7,3},{11,15},{20,16},{24,... | collective-permute-start | bytes 1769480 | tf_op jit(solution)/shard_map/ppermute | solution.py:494
  50.3 3.3 %collective-permute-start.10 = (bf16[128,1536]{1,0:T(8,128)(2,1)}, bf16[128,1536]{1,0:T(8,128)(2,1)S(1)}, u32[]{:S(2)}, u32[]{:S(2)}) collective-permute-start(bf16[128,1536]{1,0:T(8,128)(2,1)} %slice.29), channel_id=1, source_target_pairs={{4,8},{8,4},{5,9},{9,5},{6,10},{10,6},{7,11},{11,7},{20,24},{24,20... | collective-permute-start | bytes 1179656 | tf_op jit(solution)/shard_map/ppermute | solution.py:484
  53.3 1.0 slice-start.1
  53.4 2.4 slice-start
  54.3 26.3 %copy-start.7 = (bf16[128,1536]{1,0:T(8,128)(2,1)}, bf16[128,1536]{1,0:T(8,128)(2,1)S(1)}, u32[]{:S(2)}) copy-start(bf16[128,1536]{1,0:T(8,128)(2,1)S(1)} %collective-permute-done.10.refs_8_) | copy-start | bytes 1179652
  54.4 31.6 %collective-permute-start.11 = (bf16[256,1536]{1,0:T(8,128)(2,1)S(1)}, bf16[256,1536]{1,0:T(8,128)(2,1)S(1)}, u32[]{:S(2)}, u32[]{:S(2)}) collective-permute-start(bf16[256,1536]{1,0:T(8,128)(2,1)S(1)} %pad_maximum_fusion.1), channel_id=1, source_target_pairs={{4,0},{8,12},{5,1},{9,13},{6,2},{10,14},{7,3},{11,15},{20,16},{24,... | collective-permute-start | bytes 2359304 | tf_op jit(solution)/shard_map/ppermute | solution.py:499
  55.7 24.9 %copy-start.8 = (bf16[128,768]{1,0:T(8,128)(2,1)}, bf16[128,768]{1,0:T(8,128)(2,1)S(1)}, u32[]{:S(2)}) copy-start(bf16[128,768]{1,0:T(8,128)(2,1)S(1)} %collective-permute-done.6.refs_8_) | copy-start | bytes 589828
  67.6 0.8 copy-start.12
  80.6 16.4 %collective-permute-start.9 = (bf16[256,768]{1,0:T(8,128)(2,1)S(1)}, bf16[256,768]{1,0:T(8,128)(2,1)S(1)}, u32[]{:S(2)}, u32[]{:S(2)}) collective-permute-start(bf16[256,768]{1,0:T(8,128)(2,1)S(1)} %pad_maximum_fusion.2), channel_id=1, source_target_pairs={{4,0},{8,12},{5,1},{9,13},{6,2},{10,14},{7,3},{11,15},{20,16},{24,... | collective-permute-start | bytes 1179656 | tf_op jit(solution)/shard_map/ppermute | solution.py:499
  86.0 0.9 copy-start.5
  97.1 0.7 copy-start.6
  103.9 2.4 collective-permute-start.12
  106.4 11.2 %collective-permute-start.13 = (bf16[768,256]{1,0:T(8,128)(2,1)S(1)}, bf16[768,256]{1,0:T(8,128)(2,1)S(1)}, u32[]{:S(2)}, u32[]{:S(2)}) collective-permute-start(bf16[768,256]{1,0:T(8,128)(2,1)S(1)} %add_convert_fusion.8), channel_id=1, source_target_pairs={{0,2},{1,3},{2,0},{3,1},{4,6},{5,7},{6,4},{7,5},{8,10},{9,11},{10,... | collective-permute-start | bytes 1179656 | tf_op jit(solution)/shard_map/ppermute | solution.py:422
  117.7 2.4 collective-permute-start.14
  120.0 11.3 %copy-start.2 = (bf16[4608,256]{1,0:T(8,128)(2,1)S(1)}, bf16[4608,256]{1,0:T(8,128)(2,1)}, u32[]{:S(2)}) copy-start(bf16[4608,256]{1,0:T(8,128)(2,1)} %r_ref.1) | copy-start | bytes 7077892
  128.0 3.5 %collective-permute-start.16 = (f32[2,8,128]{2,1,0:T(8,128)S(1)}, f32[2,8,128]{2,1,0:T(8,128)S(1)}, u32[]{:S(2)}, u32[]{:S(2)}) collective-permute-start(f32[2,8,128]{2,1,0:T(8,128)S(1)} %get-tuple-element.58), channel_id=1, source_target_pairs={{0,1},{1,2},{2,3},{3,0},{4,5},{5,6},{6,7},{7,4},{8,9},{9,10},{10,1... | collective-permute-start | bytes 24584 | tf_op jit(solution)/shard_map/ppermute | solution.py:388
  128.2 3.3 %collective-permute-start.17 = (f32[2,8,128]{2,1,0:T(8,128)S(1)}, f32[2,8,128]{2,1,0:T(8,128)S(1)}, u32[]{:S(2)}, u32[]{:S(2)}) collective-permute-start(f32[2,8,128]{2,1,0:T(8,128)S(1)} %get-tuple-element.58), channel_id=1, source_target_pairs={{0,3},{1,0},{2,1},{3,2},{4,7},{5,4},{6,5},{7,6},{8,11},{9,8},{10,9... | collective-permute-start | bytes 24584 | tf_op jit(solution)/shard_map/ppermute | solution.py:388
  129.8 3.7 %collective-permute-start.15 = (f32[2,8,128]{2,1,0:T(8,128)S(1)}, f32[2,8,128]{2,1,0:T(8,128)S(1)}, u32[]{:S(2)}, u32[]{:S(2)}) collective-permute-start(f32[2,8,128]{2,1,0:T(8,128)S(1)} %get-tuple-element.58), channel_id=1, source_target_pairs={{0,2},{1,3},{2,0},{3,1},{4,6},{5,7},{6,4},{7,5},{8,10},{9,11},{10,... | collective-permute-start | bytes 24584 | tf_op jit(solution)/shard_map/ppermute | solution.py:388
  133.5 6.9 %copy-start = (bf16[1536,256]{1,0:T(8,128)(2,1)S(1)}, bf16[1536,256]{1,0:T(8,128)(2,1)}, u32[]{:S(2)}) copy-start(bf16[1536,256]{1,0:T(8,128)(2,1)} %refs_0_.2) | copy-start | bytes 2359300
  133.5 5.4 %collective-permute-start.18 = (f32[2,8,128]{2,1,0:T(8,128)S(1)}, f32[2,8,128]{2,1,0:T(8,128)S(1)}, u32[]{:S(2)}, u32[]{:S(2)}) collective-permute-start(f32[2,8,128]{2,1,0:T(8,128)S(1)} %add_add_fusion.1.refs_2_), channel_id=1, source_target_pairs={{0,4},{4,8},{8,12},{12,0},{1,5},{5,9},{9,13},{13,1},{2,6},{6,10},{... | collective-permute-start | bytes 24584 | tf_op jit(solution)/shard_map/ppermute | solution.py:388
  133.5 5.4 %collective-permute-start.19 = (f32[2,8,128]{2,1,0:T(8,128)S(1)}, f32[2,8,128]{2,1,0:T(8,128)S(1)}, u32[]{:S(2)}, u32[]{:S(2)}) collective-permute-start(f32[2,8,128]{2,1,0:T(8,128)S(1)} %add_add_fusion.1.refs_2_), channel_id=1, source_target_pairs={{0,8},{4,12},{8,0},{12,4},{1,9},{5,13},{9,1},{13,5},{2,10},{6,14},... | collective-permute-start | bytes 24584 | tf_op jit(solution)/shard_map/ppermute | solution.py:388
  136.7 3.7 %collective-permute-start.20 = (f32[2,8,128]{2,1,0:T(8,128)S(1)}, f32[2,8,128]{2,1,0:T(8,128)S(1)}, u32[]{:S(2)}, u32[]{:S(2)}) collective-permute-start(f32[2,8,128]{2,1,0:T(8,128)S(1)} %add_add_fusion.1.refs_2_), channel_id=1, source_target_pairs={{0,12},{4,0},{8,4},{12,8},{1,13},{5,1},{9,5},{13,9},{2,14},{6,2},{... | collective-permute-start | bytes 24584 | tf_op jit(solution)/shard_map/ppermute | solution.py:388
  137.5 3.7 %copy-start.1 = (bf16[4608,512]{1,0:T(8,128)(2,1)}, bf16[4608,512]{1,0:T(8,128)(2,1)S(1)}, u32[]{:S(2)}) copy-start(bf16[4608,512]{1,0:T(8,128)(2,1)S(1)} %constant_dynamic-update-slice_fusion.r_ref.refs_2_) | copy-start | bytes 14155780
  148.3 19.4 %collective-permute-start.21 = (bf16[256,1152]{1,0:T(8,128)(2,1)}, bf16[256,1152]{1,0:T(8,128)(2,1)}, u32[]{:S(2)}, u32[]{:S(2)}) collective-permute-start(bf16[256,1152]{1,0:T(8,128)(2,1)} %partial_pass.4.k_ref), channel_id=1, source_target_pairs={{0,4},{12,8},{1,5},{13,9},{2,6},{14,10},{3,7},{15,11},{16,20},{28,... | collective-permute-start | bytes 1769480 | tf_op jit(solution)/shard_map/ppermute | solution.py:445
  158.6 21.4 %collective-permute-start.22 = (bf16[256,1152]{1,0:T(8,128)(2,1)S(1)}, bf16[256,1152]{1,0:T(8,128)(2,1)S(1)}, u32[]{:S(2)}, u32[]{:S(2)}) collective-permute-start(bf16[256,1152]{1,0:T(8,128)(2,1)S(1)} %partial_pass.5.k_ref), channel_id=1, source_target_pairs={{0,4},{12,8},{1,5},{13,9},{2,6},{14,10},{3,7},{15,11},{16,20},{28,... | collective-permute-start | bytes 1769480 | tf_op jit(solution)/shard_map/ppermute | solution.py:445
  166.4 24.3 %collective-permute-start.24 = (bf16[256,1152]{1,0:T(8,128)(2,1)S(1)}, bf16[256,1152]{1,0:T(8,128)(2,1)S(1)}, u32[]{:S(2)}, u32[]{:S(2)}) collective-permute-start(bf16[256,1152]{1,0:T(8,128)(2,1)S(1)} %partial_pass.6), channel_id=1, source_target_pairs={{0,4},{12,8},{1,5},{13,9},{2,6},{14,10},{3,7},{15,11},{16,20},{28,... | collective-permute-start | bytes 1769480 | tf_op jit(solution)/shard_map/ppermute | solution.py:445
  169.1 11.7 %collective-permute-start.23 = (bf16[256,1152]{1,0:T(8,128)(2,1)S(1)}, bf16[256,1152]{1,0:T(8,128)(2,1)S(1)}, u32[]{:S(2)}, u32[]{:S(2)}) collective-permute-start(bf16[256,1152]{1,0:T(8,128)(2,1)S(1)} %add_convert_fusion.7.k_ref), channel_id=1, source_target_pairs={{4,8},{8,4},{5,9},{9,5},{6,10},{10,6},{7,11},{11,7},{20,24},{24,20... | collective-permute-start | bytes 1769480 | tf_op jit(solution)/shard_map/ppermute | solution.py:451
  176.3 23.9 %collective-permute-start.26 = (bf16[256,1152]{1,0:T(8,128)(2,1)S(1)}, bf16[256,1152]{1,0:T(8,128)(2,1)S(1)}, u32[]{:S(2)}, u32[]{:S(2)}) collective-permute-start(bf16[256,1152]{1,0:T(8,128)(2,1)S(1)} %partial_pass.7), channel_id=1, source_target_pairs={{0,4},{12,8},{1,5},{13,9},{2,6},{14,10},{3,7},{15,11},{16,20},{28,... | collective-permute-start | bytes 1769480 | tf_op jit(solution)/shard_map/ppermute | solution.py:445
  180.1 11.4 %collective-permute-start.25 = (bf16[256,1152]{1,0:T(8,128)(2,1)S(1)}, bf16[256,1152]{1,0:T(8,128)(2,1)S(1)}, u32[]{:S(2)}, u32[]{:S(2)}) collective-permute-start(bf16[256,1152]{1,0:T(8,128)(2,1)S(1)} %add_convert_fusion.6), channel_id=1, source_target_pairs={{4,8},{8,4},{5,9},{9,5},{6,10},{10,6},{7,11},{11,7},{20,24},{24,20... | collective-permute-start | bytes 1769480 | tf_op jit(solution)/shard_map/ppermute | solution.py:451
  181.0 20.1 %collective-permute-start.27 = (bf16[256,1152]{1,0:T(8,128)(2,1)S(1)}, bf16[256,1152]{1,0:T(8,128)(2,1)S(1)}, u32[]{:S(2)}, u32[]{:S(2)}) collective-permute-start(bf16[256,1152]{1,0:T(8,128)(2,1)S(1)} %add_convert_fusion.5.t_ref), channel_id=1, source_target_pairs={{4,0},{8,12},{5,1},{9,13},{6,2},{10,14},{7,3},{11,15},{20,16},{24,... | collective-permute-start | bytes 1769480 | tf_op jit(solution)/shard_map/ppermute | solution.py:457
  190.8 13.6 %collective-permute-start.28 = (bf16[256,1152]{1,0:T(8,128)(2,1)S(1)}, bf16[256,1152]{1,0:T(8,128)(2,1)S(1)}, u32[]{:S(2)}, u32[]{:S(2)}) collective-permute-start(bf16[256,1152]{1,0:T(8,128)(2,1)S(1)} %add_convert_fusion.4), channel_id=1, source_target_pairs={{4,8},{8,4},{5,9},{9,5},{6,10},{10,6},{7,11},{11,7},{20,24},{24,20... | collective-permute-start | bytes 1769480 | tf_op jit(solution)/shard_map/ppermute | solution.py:451
  191.6 16.7 %collective-permute-start.29 = (bf16[256,1152]{1,0:T(8,128)(2,1)S(1)}, bf16[256,1152]{1,0:T(8,128)(2,1)S(1)}, u32[]{:S(2)}, u32[]{:S(2)}) collective-permute-start(bf16[256,1152]{1,0:T(8,128)(2,1)S(1)} %add_convert_fusion.3.t_ref), channel_id=1, source_target_pairs={{4,0},{8,12},{5,1},{9,13},{6,2},{10,14},{7,3},{11,15},{20,16},{24,... | collective-permute-start | bytes 1769480 | tf_op jit(solution)/shard_map/ppermute | solution.py:457
  200.3 11.3 %collective-permute-start.30 = (bf16[256,1152]{1,0:T(8,128)(2,1)S(1)}, bf16[256,1152]{1,0:T(8,128)(2,1)S(1)}, u32[]{:S(2)}, u32[]{:S(2)}) collective-permute-start(bf16[256,1152]{1,0:T(8,128)(2,1)S(1)} %add_convert_fusion.2), channel_id=1, source_target_pairs={{4,8},{8,4},{5,9},{9,5},{6,10},{10,6},{7,11},{11,7},{20,24},{24,20... | collective-permute-start | bytes 1769480 | tf_op jit(solution)/shard_map/ppermute | solution.py:451
  204.6 16.7 %collective-permute-start.31 = (bf16[256,1152]{1,0:T(8,128)(2,1)S(1)}, bf16[256,1152]{1,0:T(8,128)(2,1)S(1)}, u32[]{:S(2)}, u32[]{:S(2)}) collective-permute-start(bf16[256,1152]{1,0:T(8,128)(2,1)S(1)} %add_convert_fusion.1.t_ref), channel_id=1, source_target_pairs={{4,0},{8,12},{5,1},{9,13},{6,2},{10,14},{7,3},{11,15},{20,16},{24,... | collective-permute-start | bytes 1769480 | tf_op jit(solution)/shard_map/ppermute | solution.py:457
  211.8 21.5 %collective-permute-start.32 = (bf16[256,1152]{1,0:T(8,128)(2,1)S(1)}, bf16[256,1152]{1,0:T(8,128)(2,1)S(1)}, u32[]{:S(2)}, u32[]{:S(2)}) collective-permute-start(bf16[256,1152]{1,0:T(8,128)(2,1)S(1)} %add_convert_fusion.t_ref), channel_id=1, source_target_pairs={{4,0},{8,12},{5,1},{9,13},{6,2},{10,14},{7,3},{11,15},{20,16},{24,... | collective-permute-start | bytes 1769480 | tf_op jit(solution)/shard_map/ppermute | solution.py:457
  236.7 3.2 %collective-permute-start.34 = (f32[2,8,128]{2,1,0:T(8,128)S(1)}, f32[2,8,128]{2,1,0:T(8,128)S(1)}, u32[]{:S(2)}, u32[]{:S(2)}) collective-permute-start(f32[2,8,128]{2,1,0:T(8,128)S(1)} %get-tuple-element.82), channel_id=1, source_target_pairs={{0,1},{1,2},{2,3},{3,0},{4,5},{5,6},{6,7},{7,4},{8,9},{9,10},{10,1... | collective-permute-start | bytes 24584 | tf_op jit(solution)/shard_map/ppermute | solution.py:388
  236.8 3.1 %collective-permute-start.35 = (f32[2,8,128]{2,1,0:T(8,128)S(1)}, f32[2,8,128]{2,1,0:T(8,128)S(1)}, u32[]{:S(2)}, u32[]{:S(2)}) collective-permute-start(f32[2,8,128]{2,1,0:T(8,128)S(1)} %get-tuple-element.82), channel_id=1, source_target_pairs={{0,3},{1,0},{2,1},{3,2},{4,7},{5,4},{6,5},{7,6},{8,11},{9,8},{10,9... | collective-permute-start | bytes 24584 | tf_op jit(solution)/shard_map/ppermute | solution.py:388
  238.5 3.7 %collective-permute-start.33 = (f32[2,8,128]{2,1,0:T(8,128)S(1)}, f32[2,8,128]{2,1,0:T(8,128)S(1)}, u32[]{:S(2)}, u32[]{:S(2)}) collective-permute-start(f32[2,8,128]{2,1,0:T(8,128)S(1)} %get-tuple-element.82), channel_id=1, source_target_pairs={{0,2},{1,3},{2,0},{3,1},{4,6},{5,7},{6,4},{7,5},{8,10},{9,11},{10,... | collective-permute-start | bytes 24584 | tf_op jit(solution)/shard_map/ppermute | solution.py:388
  242.2 5.5 %collective-permute-start.36 = (f32[2,8,128]{2,1,0:T(8,128)S(1)}, f32[2,8,128]{2,1,0:T(8,128)S(1)}, u32[]{:S(2)}, u32[]{:S(2)}) collective-permute-start(f32[2,8,128]{2,1,0:T(8,128)S(1)} %add_add_fusion.refs_8_), channel_id=1, source_target_pairs={{0,4},{4,8},{8,12},{12,0},{1,5},{5,9},{9,13},{13,1},{2,6},{6,10},{... | collective-permute-start | bytes 24584 | tf_op jit(solution)/shard_map/ppermute | solution.py:388
  242.2 5.5 %collective-permute-start.37 = (f32[2,8,128]{2,1,0:T(8,128)S(1)}, f32[2,8,128]{2,1,0:T(8,128)S(1)}, u32[]{:S(2)}, u32[]{:S(2)}) collective-permute-start(f32[2,8,128]{2,1,0:T(8,128)S(1)} %add_add_fusion.refs_8_), channel_id=1, source_target_pairs={{0,8},{4,12},{8,0},{12,4},{1,9},{5,13},{9,1},{13,5},{2,10},{6,14},... | collective-permute-start | bytes 24584 | tf_op jit(solution)/shard_map/ppermute | solution.py:388
  244.7 3.7 %collective-permute-start.38 = (f32[2,8,128]{2,1,0:T(8,128)S(1)}, f32[2,8,128]{2,1,0:T(8,128)S(1)}, u32[]{:S(2)}, u32[]{:S(2)}) collective-permute-start(f32[2,8,128]{2,1,0:T(8,128)S(1)} %add_add_fusion.refs_8_), channel_id=1, source_target_pairs={{0,12},{4,0},{8,4},{12,8},{1,13},{5,1},{9,5},{13,9},{2,14},{6,2},{... | collective-permute-start | bytes 24584 | tf_op jit(solution)/shard_map/ppermute | solution.py:388

commit v2 on v1

--- a/solution.py
+++ b/solution.py
@@ -261,13 +261,19 @@
     )(left, near(descent), *pieces)
 
 
+def moved_image(p_ref, rows, r_ref):
+    rank = r_ref.shape[1]
+    high = lax.dot_general(p_ref[rows, :rank], r_ref[...], NT, preferred_element_type=f32)
+    return high + lax.dot_general(p_ref[rows, rank:], r_ref[...], NT, preferred_element_type=f32)
+
+
 def partial_kernel(tile, p_ref, w_ref, r_ref, f_ref, t_ref, k_ref, o_ref, acc_ref):
     m = p_ref.shape[0]
     acc_ref[...] = jnp.zeros_like(acc_ref)
 
     def step_rows(i):
         rows = span(i, tile)
-        image = lax.dot_general(p_ref[rows, :], r_ref[...], NT, preferred_element_type=f32)
+        image = moved_image(p_ref, rows, r_ref)
         later = w_ref[rows, :].astype(f32) - image
         weighted = (f_ref[rows, :].astype(f32) * later).astype(bf16)
         acc_ref[...] += jnp.dot(t_ref[:, rows], weighted, preferred_element_type=f32)
@@ -275,7 +281,7 @@
     o_ref[...] = acc_ref[...].astype(o_ref.dtype)
 
 
-def partial_pass(pair, w, twice, f, new_t, token, offset, width):
+def partial_pass(pair, w, right, f, new_t, token, offset, width):
     m, n = w.shape
     rank = new_t.shape[0]
     bn = pick(width, WIDE, offset)
@@ -286,7 +292,7 @@
         functools.partial(partial_kernel, tile),
         grid=(width // bn,),
         in_specs=[pl.BlockSpec((m, 2 * rank), lambda j: (0, 0)), wide,
-                  pl.BlockSpec((bn, 2 * rank), lambda j: (base + j, 0)), wide,
+                  pl.BlockSpec((bn, rank), lambda j: (base + j, 0)), wide,
                   pl.BlockSpec((rank, m), lambda j: (0, 0)), pl.BlockSpec(memory_space=pl.ANY)],
         out_specs=pl.BlockSpec((rank, bn), lambda j: (0, j)),
         out_shape=jax.ShapeDtypeStruct((rank, width), bf16),
@@ -294,7 +300,7 @@
         compiler_params=pltpu.CompilerParams(vmem_limit_bytes=LIMIT),
         cost_estimate=pl.CostEstimate(flops=6 * m * width * rank, bytes_accessed=4 * m * width, transcendentals=0),
         name="partial_pass",
-    )(near(pair), far(w), far(twice), far(f), near(new_t), token)
+    )(near(pair), far(w), far(right), far(f), near(new_t), token)
 
 
 def last_kernel(tile, copies, edges, *refs):
@@ -305,7 +311,6 @@
     j = pl.program_id(0)
     s2 = step_of(total_of(pieces), copies)
     m = p_ref.shape[0]
-    rank = n_ref.shape[1]
     for (first, count), ref in zip(edges, q_refs):
         @pl.when((j >= first) & (j < first + count))
         def _():
@@ -313,15 +318,15 @@
 
     def step_rows(i):
         rows = span(i, tile)
-        image = lax.dot_general(p_ref[rows, :], r_ref[...], NT, preferred_element_type=f32)
+        image = moved_image(p_ref, rows, r_ref)
         second = jnp.dot(n_ref[rows, :], q_ref[...], preferred_element_type=f32)
         later = w_ref[rows, :].astype(f32) - image
         o_ref[rows, :] = (later - s2 * second).astype(o_ref.dtype)
     each(m // tile, UNROLL, step_rows)
-    new_ref[...] = (r_ref[:, :rank].astype(f32) + s2 * q_ref[...].astype(f32).T).astype(bf16)
-
-
-def last_pass(w, pair, twice, left_new, parts, pieces, copies):
+    new_ref[...] = (r_ref[...].astype(f32) + s2 * q_ref[...].astype(f32).T).astype(bf16)
+
+
+def last_pass(w, pair, right, left_new, parts, pieces, copies):
     m, n = w.shape
     rank = left_new.shape[1]
     common = n
@@ -343,7 +348,7 @@
     return pl.pallas_call(
         functools.partial(last_kernel, pick(m, TILE), copies, tuple(edges)),
         grid=(n // bn,),
-        in_specs=[wide, pl.BlockSpec((m, 2 * rank), lambda j: (0, 0)), pl.BlockSpec((bn, 2 * rank), lambda j: (j, 0)), whole]
+        in_specs=[wide, pl.BlockSpec((m, 2 * rank), lambda j: (0, 0)), pl.BlockSpec((bn, rank), lambda j: (j, 0)), whole]
         + [tall(*edge) for edge in edges]
         + [pl.BlockSpec((2, 8, 128), lambda j: (0, 0, 0))] * len(pieces),
         out_specs=[wide, side],
@@ -352,7 +357,7 @@
         compiler_params=pltpu.CompilerParams(vmem_limit_bytes=LIMIT),
         cost_estimate=pl.CostEstimate(flops=6 * m * n * rank, bytes_accessed=4 * m * n, transcendentals=0),
         name="last_pass",
-    )(far(w), near(pair), far(twice), left_new, *parts, *pieces)
+    )(far(w), near(pair), far(right), left_new, *parts, *pieces)
 
 
 FIRST = (3, 2, 1)
@@ -467,7 +472,6 @@
     m, n = matrix.shape
     shard = out_grads.shape[0]
     line = row_count == 4 and col_count == 4
-    twice = jnp.concatenate([right, right], axis=1)
     prev = None
     if line:
         outward = [(0, 1), (1, 0), (2, 3), (3, 2)]
@@ -519,7 +523,7 @@
     parts = [None] * len(chunks)
 
     def make(k, token):
-        return partial_pass(pair, matrix, twice, fisher, new_t, step if token is None else token, *chunks[k])
+        return partial_pass(pair, matrix, right, fisher, new_t, step if token is None else token, *chunks[k])
 
     def finish(k, total, back, token):
         nonlocal sums
@@ -535,7 +539,7 @@
             total = lax.psum(make(k, None), "row")
             finish(k, total, total, None)
     pieces = pieces_of(add_up(sums, "col"), "row")
-    residual, right_new = last_pass(matrix, pair, twice, left_new, parts, pieces, row_count)
+    residual, right_new = last_pass(matrix, pair, right, left_new, parts, pieces, row_count)
     return (left_new, right_new, residual)
 
 

time: 269 us -> 268 us (level)
  no operation moved by 1% of the time
where the time goes in v2:
time: 268 us; the launch traced here: 267 us
  waiting for transfers between devices  112 us (42%)
  Pallas kernels  96 us (36%)
  starting transfers between devices  47.8 us (18%)
  local copies, waits for them, and re-layouts  6.07 us (2%)
  other arithmetic  4.22 us (2%)
    pallas_call x3, Pallas kernels, first_pass(): pl.pallas_call(functools.partial(first_kernel, tuple((len(g) for g in gro...  28.4 us
    pallas_call x4, Pallas kernels, partial_pass(): pl.pallas_call(functools.partial(partial_kernel, tile), grid=(width // bn...  26.3 us
    ppermute x1, waiting for transfers between devices, body(): outer = lax.ppermute(out_grads, 'row', outward)  23.9 us
    ppermute x4, waiting for transfers between devices, back(): backs[k] = lax.ppermute(totals[k], axis, [(1, 0), (2, 3)])  19.3 us
    pallas_call x1, Pallas kernels, last_pass(): pl.pallas_call(functools.partial(last_kernel, pick(m, TILE), copies, tupl...  19.3 us
    ppermute x4, waiting for transfers between devices, half(): came = lax.ppermute(sent[k], axis, [(0, 1), (3, 2)])  15.6 us
    ppermute x1, waiting for transfers between devices, body(): early = lax.ppermute(inners[0], 'row', onward)  14.4 us
    ppermute x12, starting transfers between devices, pieces_of(): return [x] + [lax.ppermute(x, axis, turned(4, k)) for k in (1, 2, 3)]  14.1 us
  transfers between devices with their start and end apart: 39, of which 18 were waited for; matrix products, arithmetic and copies ran while one was open for 3% of the time, Pallas kernels for 19%

profile of v2, /device:TPU:0, one launch (start us, length us, event | category | flops | bytes accessed | tf_op | source)
XLA Modules:
  0.0 267.5 jit_solution(15113959979746574523)
XLA Ops:
  0.6 3.1 %collective-permute-start.2 = (bf16[128,4608]{1,0:T(8,128)(2,1)}, bf16[128,4608]{1,0:T(8,128)(2,1)S(1)}, u32[]{:S(2)}, u32[]{:S(2)}) collective-permute-start(bf16[128,4608]{1,0:T(8,128)(2,1)} %refs_4_.5), channel_id=1, source_target_pairs={{0,4},{4,0},{8,12},{12,8},{1,5},{5,1},{9,13},{13,9},{2,6},{6,2},{1... | collective-permute-start | bytes 3538952 | tf_op jit(solution)/shard_map/ppermute | solution.py:480
  3.7 0.7 collective-permute-start.5
  4.5 1.6 collective-permute-start.1
  6.0 23.9 %collective-permute-done.2.refs_5_ = bf16[128,4608]{1,0:T(8,128)(2,1)S(1)} collective-permute-done((bf16[128,4608]{1,0:T(8,128)(2,1)}, bf16[128,4608]{1,0:T(8,128)(2,1)S(1)}, u32[]{:S(2)}, u32[]{:S(2)}) %collective-permute-start.2) | collective-permute-done | bytes 1179680 | tf_op jit(solution)/shard_map/ppermute | solution.py:480
  30.0 1.6 collective-permute-start.3
  31.7 1.3 collective-permute-start.7
  33.1 0.8 slice.29
  34.6 14.4 %collective-permute-done.7.refs_7_ = bf16[128,2304]{1,0:T(8,128)(2,1)} collective-permute-done((bf16[128,2304]{1,0:T(8,128)(2,1)S(1)}, bf16[128,2304]{1,0:T(8,128)(2,1)}, u32[]{:S(2)}, u32[]{:S(2)}) %collective-permute-start.7) | collective-permute-done | bytes 589856 | tf_op jit(solution)/shard_map/ppermute | solution.py:497
  49.0 1.3 collective-permute-start.8
  51.0 1.3 pad_maximum_fusion
  53.6 0.8 slice-done.1
  54.4 1.3 collective-permute-start.11
  55.8 11.8 %collective-permute-done.8.refs_9_ = bf16[128,2304]{1,0:T(8,128)(2,1)S(1)} collective-permute-done((bf16[128,2304]{1,0:T(8,128)(2,1)}, bf16[128,2304]{1,0:T(8,128)(2,1)S(1)}, u32[]{:S(2)}, u32[]{:S(2)}) %collective-permute-start.8) | collective-permute-done | bytes 589856 | tf_op jit(solution)/shard_map/ppermute | solution.py:498
  67.6 0.8 copy-done.10
  68.4 12.3 %first_pass.3 = (bf16[1536,4608]{1,0:T(8,128)(2,1)}, f32[1536,256]{1,0:T(8,128)S(1)}) custom-call(bf16[1536,512]{1,0:T(8,128)(2,1)S(1)} %maximum_bitcast_fusion.refs_0_, bf16[1536,4608]{1,0:T(8,128)(2,1)} %refs_0_.3, bf16[1536,256]{1,0:T(8,128)(2,1)} %refs_0_.2, bf16[4608,256]{1,0:T(8,128)(2,1)} %refs_2_.7, bf16[128,4608]{1,0:T(8,128)(2,1)} %refs_4_.5, ...), custom_call_target="tpu_custom_call" | custom-call | flops 7247757312 | bytes 14155776 | tf_op jit(solution)/shard_map/first_pass/pallas_call | solution.py:129
  80.6 1.5 collective-permute-start.9
  82.1 3.9 %collective-permute-done.11.refs_7_.refs_9_ = bf16[256,1536]{1,0:T(8,128)(2,1)S(1)} collective-permute-done((bf16[256,1536]{1,0:T(8,128)(2,1)S(1)}, bf16[256,1536]{1,0:T(8,128)(2,1)S(1)}, u32[]{:S(2)}, u32[]{:S(2)}) %collective-permute-start.11) | collective-permute-done | bytes 786464 | tf_op jit(solution)/shard_map/ppermute | solution.py:503
  86.0 0.9 copy-done.3
  86.9 10.2 %first_pass.4 = (bf16[1536,4608]{1,0:T(8,128)(2,1)}, f32[1536,256]{1,0:T(8,128)S(1)}) custom-call(bf16[1536,512]{1,0:T(8,128)(2,1)S(1)} %maximum_bitcast_fusion.refs_0_, bf16[1536,4608]{1,0:T(8,128)(2,1)} %refs_0_.3, bf16[1536,256]{1,0:T(8,128)(2,1)} %refs_0_.2, bf16[4608,256]{1,0:T(8,128)(2,1)} %refs_2_.7, ...), custom_call_target="tpu_custom_call", output_to_operand_aliasing={{1}: (10, {}), {0}: (11, {})} | custom-call | flops 4831838208 | bytes 9437184 | tf_op jit(solution)/shard_map/first_pass/pallas_call | solution.py:129
  97.1 0.7 copy-done.4
  97.8 6.0 %first_pass.5 = (bf16[1536,4608]{1,0:T(8,128)(2,1)}, f32[1536,256]{1,0:T(8,128)S(1)}) custom-call(bf16[1536,512]{1,0:T(8,128)(2,1)S(1)} %maximum_bitcast_fusion.refs_0_, bf16[1536,4608]{1,0:T(8,128)(2,1)} %refs_0_.3, bf16[1536,256]{1,0:T(8,128)(2,1)} %refs_0_.2, bf16[4608,256]{1,0:T(8,128)(2,1)} %refs_2_.7, ...), custom_call_target="tpu_custom_call", output_to_operand_aliasing={{1}: (10, {}), {0}: (11, {})} | custom-call | flops 2415919104 | bytes 4718592 | tf_op jit(solution)/shard_map/first_pass/pallas_call | solution.py:129
  104.0 2.3 collective-permute-done.12
  106.4 1.6 collective-permute-start.13
  107.9 9.7 %collective-permute-done.13 = bf16[768,256]{1,0:T(8,128)(2,1)S(1)} collective-permute-done((bf16[768,256]{1,0:T(8,128)(2,1)S(1)}, bf16[768,256]{1,0:T(8,128)(2,1)S(1)}, u32[]{:S(2)}, u32[]{:S(2)}) %collective-permute-start.13) | collective-permute-done | bytes 393248 | tf_op jit(solution)/shard_map/ppermute | solution.py:427
  117.8 2.3 collective-permute-done.14.c_ref
  120.0 7.9 %left_curve.1 = (f32[2,8,128]{2,1,0:T(8,128)S(1)}, f32[1536,256]{1,0:T(8,128)S(1)}) custom-call(s32[1,1]{1,0:T(1,128)} %bitcast.side_ref, f32[768,256]{1,0:T(8,128)S(1)} %convert_add_fusion.b_ref, f32[768,256]{1,0:T(8,128)S(1)} %collective-permute-done.14.c_ref, bf16[4608,256]{1,0:T(8,128)(2,1)} %refs_2_.7, bf16[1536,4608]{1,0:T(8,128)(2,1)} %get-tuple-element.56.f_ref), custom_call_target="tpu_custom_call" | custom-call | flops 3623878656 | bytes 14155776 | tf_op jit(solution)/shard_map/left_curve/pallas_call | solution.py:183
  128.1 1.6 collective-permute-start.17
  129.7 1.5 collective-permute-start.15
  131.2 2.2 collective-permute-done.15
  133.4 3.3 %collective-permute-start.19 = (f32[2,8,128]{2,1,0:T(8,128)S(1)}, f32[2,8,128]{2,1,0:T(8,128)S(1)}, u32[]{:S(2)}, u32[]{:S(2)}) collective-permute-start(f32[2,8,128]{2,1,0:T(8,128)S(1)} %add_add_fusion.1.refs_2_), channel_id=1, source_target_pairs={{0,8},{4,12},{8,0},{12,4},{1,9},{5,13},{9,1},{13,5},{2,10},{6,14},... | collective-permute-start | bytes 24584 | tf_op jit(solution)/shard_map/ppermute | solution.py:393
  137.2 1.6 collective-permute-done.18.refs_3_
  138.8 1.5 collective-permute-done.20.refs_5_
  140.3 0.8 left_update.1
  141.1 7.1 %partial_pass.4.k_ref = bf16[256,1152]{1,0:T(8,128)(2,1)} custom-call(bf16[1536,512]{1,0:T(8,128)(2,1)S(1)} %get-tuple-element.60.p_ref.refs_1_, bf16[1536,4608]{1,0:T(8,128)(2,1)} %refs_0_.3, bf16[4608,256]{1,0:T(8,128)(2,1)} %refs_2_.7, bf16[1536,4608]{1,0:T(8,128)(2,1)} %get-tuple-element.56.f_ref, bf16[256,1536]{1,0:T(8,128)(2,1)S(1)} %get-tuple-element.61.t_ref, ...), custom_call_target="tpu_custom_call" | custom-call | flops 2717908992 | bytes 7077888 | tf_op jit(solution)/shard_map/partial_pass/pallas_call | solution.py:291
  148.2 3.9 %collective-permute-start.21 = (bf16[256,1152]{1,0:T(8,128)(2,1)}, bf16[256,1152]{1,0:T(8,128)(2,1)}, u32[]{:S(2)}, u32[]{:S(2)}) collective-permute-start(bf16[256,1152]{1,0:T(8,128)(2,1)} %partial_pass.4.k_ref), channel_id=1, source_target_pairs={{0,4},{12,8},{1,5},{13,9},{2,6},{14,10},{3,7},{15,11},{16,20},{28,... | collective-permute-start | bytes 1769480 | tf_op jit(solution)/shard_map/ppermute | solution.py:450
  152.1 6.4 %partial_pass.5.k_ref = bf16[256,1152]{1,0:T(8,128)(2,1)S(1)} custom-call(bf16[1536,512]{1,0:T(8,128)(2,1)S(1)} %get-tuple-element.60.p_ref.refs_1_, bf16[1536,4608]{1,0:T(8,128)(2,1)} %refs_0_.3, bf16[4608,256]{1,0:T(8,128)(2,1)} %refs_2_.7, bf16[1536,4608]{1,0:T(8,128)(2,1)} %get-tuple-element.56.f_ref, bf16[256,1536]{1,0:T(8,128)(2,1)S(1)} %get-tuple-element.61.t_ref, ...), custom_call_target="tpu_custom_call" | custom-call | flops 2717908992 | bytes 7077888 | tf_op jit(solution)/shard_map/partial_pass/pallas_call | solution.py:291
  158.5 1.3 collective-permute-start.22
  159.8 6.4 %partial_pass.6 = bf16[256,1152]{1,0:T(8,128)(2,1)S(1)} custom-call(bf16[1536,512]{1,0:T(8,128)(2,1)S(1)} %get-tuple-element.60.p_ref.refs_1_, bf16[1536,4608]{1,0:T(8,128)(2,1)} %refs_0_.3, bf16[4608,256]{1,0:T(8,128)(2,1)} %refs_2_.7, bf16[1536,4608]{1,0:T(8,128)(2,1)} %get-tuple-element.56.f_ref, bf16[256,1536]{1,0:T(8,128)(2,1)S(1)} %get-tuple-element.61.t_ref, ...), custom_call_target="tpu_custom_call" | custom-call | flops 2717908992 | bytes 7077888 | tf_op jit(solution)/shard_map/partial_pass/pallas_call | solution.py:291
  166.2 1.3 collective-permute-start.24
  167.5 1.4 add_convert_fusion.7.k_ref
  168.9 0.7 collective-permute-start.23
  169.6 6.4 %partial_pass.7 = bf16[256,1152]{1,0:T(8,128)(2,1)S(1)} custom-call(bf16[1536,512]{1,0:T(8,128)(2,1)S(1)} %get-tuple-element.60.p_ref.refs_1_, bf16[1536,4608]{1,0:T(8,128)(2,1)} %refs_0_.3, bf16[4608,256]{1,0:T(8,128)(2,1)} %refs_2_.7, bf16[1536,4608]{1,0:T(8,128)(2,1)} %get-tuple-element.56.f_ref, bf16[256,1536]{1,0:T(8,128)(2,1)S(1)} %get-tuple-element.61.t_ref, ...), custom_call_target="tpu_custom_call" | custom-call | flops 2717908992 | bytes 7077888 | tf_op jit(solution)/shard_map/partial_pass/pallas_call | solution.py:291
  176.1 3.7 %collective-permute-start.26 = (bf16[256,1152]{1,0:T(8,128)(2,1)S(1)}, bf16[256,1152]{1,0:T(8,128)(2,1)S(1)}, u32[]{:S(2)}, u32[]{:S(2)}) collective-permute-start(bf16[256,1152]{1,0:T(8,128)(2,1)S(1)} %partial_pass.7), channel_id=1, source_target_pairs={{0,4},{12,8},{1,5},{13,9},{2,6},{14,10},{3,7},{15,11},{16,20},{28,... | collective-permute-start | bytes 1769480 | tf_op jit(solution)/shard_map/ppermute | solution.py:450
  180.8 1.3 collective-permute-start.27
  182.1 8.4 %collective-permute-done.24 = bf16[256,1152]{1,0:T(8,128)(2,1)S(1)} collective-permute-done((bf16[256,1152]{1,0:T(8,128)(2,1)S(1)}, bf16[256,1152]{1,0:T(8,128)(2,1)S(1)}, u32[]{:S(2)}, u32[]{:S(2)}) %collective-permute-start.24) | collective-permute-done | bytes 589856 | tf_op jit(solution)/shard_map/ppermute | solution.py:450
  191.5 1.3 collective-permute-start.29
  192.8 7.2 %collective-permute-done.26 = bf16[256,1152]{1,0:T(8,128)(2,1)S(1)} collective-permute-done((bf16[256,1152]{1,0:T(8,128)(2,1)S(1)}, bf16[256,1152]{1,0:T(8,128)(2,1)S(1)}, u32[]{:S(2)}, u32[]{:S(2)}) %collective-permute-start.26) | collective-permute-done | bytes 589856 | tf_op jit(solution)/shard_map/ppermute | solution.py:450
  200.9 3.3 %right_curve.4 = (f32[2,8,128]{2,1,0:T(8,128)S(1)}, bf16[256,1152]{1,0:T(8,128)(2,1)S(1)}) custom-call(s32[1,1]{1,0:T(1,128)} %bitcast.10.flag_ref, bf16[1536,256]{1,0:T(8,128)(2,1)S(1)} %get-tuple-element.89.a_ref.refs_3_, bf16[256,1152]{1,0:T(8,128)(2,1)S(1)} %add_convert_fusion.5.t_ref, bf16[256,1152]{1,0:T(8,128)(2,1)S(1)} %collective-permute-done.27.b_ref, ...), custom_call_target="tpu_custom_call" | custom-call | flops 905969664 | bytes 3538944 | tf_op jit(solution)/shard_map/right_curve/pallas_call | solution.py:222
  204.4 1.3 collective-permute-start.31
  205.7 2.8 %collective-permute-done.29.b_ref = bf16[256,1152]{1,0:T(8,128)(2,1)S(1)} collective-permute-done((bf16[256,1152]{1,0:T(8,128)(2,1)S(1)}, bf16[256,1152]{1,0:T(8,128)(2,1)S(1)}, u32[]{:S(2)}, u32[]{:S(2)}) %collective-permute-start.29) | collective-permute-done | bytes 589856 | tf_op jit(solution)/shard_map/ppermute | solution.py:462
  208.5 3.3 %right_curve.5 = (f32[2,8,128]{2,1,0:T(8,128)S(1)}, bf16[256,1152]{1,0:T(8,128)(2,1)S(1)}) custom-call(s32[1,1]{1,0:T(1,128)} %bitcast.10.flag_ref, bf16[1536,256]{1,0:T(8,128)(2,1)S(1)} %get-tuple-element.89.a_ref.refs_3_, bf16[256,1152]{1,0:T(8,128)(2,1)S(1)} %add_convert_fusion.3.t_ref, bf16[256,1152]{1,0:T(8,128)(2,1)S(1)} %collective-permute-done.29.b_ref, ...), custom_call_target="tpu_custom_call" | custom-call | flops 905969664 | bytes 3538944 | tf_op jit(solution)/shard_map/right_curve/pallas_call | solution.py:222
  212.0 1.3 collective-permute-start.32
  213.3 7.9 %collective-permute-done.31.b_ref = bf16[256,1152]{1,0:T(8,128)(2,1)S(1)} collective-permute-done((bf16[256,1152]{1,0:T(8,128)(2,1)S(1)}, bf16[256,1152]{1,0:T(8,128)(2,1)S(1)}, u32[]{:S(2)}, u32[]{:S(2)}) %collective-permute-start.31) | collective-permute-done | bytes 589856 | tf_op jit(solution)/shard_map/ppermute | solution.py:462
  221.2 3.3 %right_curve.6 = (f32[2,8,128]{2,1,0:T(8,128)S(1)}, bf16[256,1152]{1,0:T(8,128)(2,1)S(1)}) custom-call(s32[1,1]{1,0:T(1,128)} %bitcast.10.flag_ref, bf16[1536,256]{1,0:T(8,128)(2,1)S(1)} %get-tuple-element.89.a_ref.refs_3_, bf16[256,1152]{1,0:T(8,128)(2,1)S(1)} %add_convert_fusion.1.t_ref, bf16[256,1152]{1,0:T(8,128)(2,1)S(1)} %collective-permute-done.31.b_ref, ...), custom_call_target="tpu_custom_call" | custom-call | flops 905969664 | bytes 3538944 | tf_op jit(solution)/shard_map/right_curve/pallas_call | solution.py:222
  224.6 8.6 %collective-permute-done.32.b_ref = bf16[256,1152]{1,0:T(8,128)(2,1)S(1)} collective-permute-done((bf16[256,1152]{1,0:T(8,128)(2,1)S(1)}, bf16[256,1152]{1,0:T(8,128)(2,1)S(1)}, u32[]{:S(2)}, u32[]{:S(2)}) %collective-permute-start.32) | collective-permute-done | bytes 589856 | tf_op jit(solution)/shard_map/ppermute | solution.py:462
  233.2 3.4 %right_curve.7 = (f32[2,8,128]{2,1,0:T(8,128)S(1)}, bf16[256,1152]{1,0:T(8,128)(2,1)S(1)}) custom-call(s32[1,1]{1,0:T(1,128)} %bitcast.10.flag_ref, bf16[1536,256]{1,0:T(8,128)(2,1)S(1)} %get-tuple-element.89.a_ref.refs_3_, bf16[256,1152]{1,0:T(8,128)(2,1)S(1)} %add_convert_fusion.t_ref, bf16[256,1152]{1,0:T(8,128)(2,1)S(1)} %collective-permute-done.32.b_ref, ...), custom_call_target="tpu_custom_call" | custom-call | flops 905969664 | bytes 3538944 | tf_op jit(solution)/shard_map/right_curve/pallas_call | solution.py:222
  236.6 1.7 collective-permute-start.35
  238.4 1.4 collective-permute-start.33
  239.7 2.3 collective-permute-done.33
  242.0 2.5 collective-permute-start.37
  244.5 1.3 collective-permute-start.38
  245.8 0.9 copy.20
  246.7 0.8 collective-permute-done.36.refs_9_
  248.2 19.3 %last_pass.1 = (bf16[1536,4608]{1,0:T(8,128)(2,1)}, bf16[4608,256]{1,0:T(8,128)(2,1)}) custom-call(bf16[1536,4608]{1,0:T(8,128)(2,1)} %refs_0_.3, bf16[1536,512]{1,0:T(8,128)(2,1)S(1)} %get-tuple-element.60.p_ref.refs_1_, bf16[4608,256]{1,0:T(8,128)(2,1)} %refs_2_.7, bf16[1536,256]{1,0:T(8,128)(2,1)S(1)} %get-tuple-element.89.a_ref.refs_3_, ...), custom_call_target="tpu_custom_call" | custom-call | flops 10871635968 | bytes 28311552 | tf_op jit(solution)/shard_map/last_pass/pallas_call | solution.py:348
  (82 shorter events, 7.9 us)
Async XLA Ops:
  0.6 29.3 %collective-permute-start.2 = (bf16[128,4608]{1,0:T(8,128)(2,1)}, bf16[128,4608]{1,0:T(8,128)(2,1)S(1)}, u32[]{:S(2)}, u32[]{:S(2)}) collective-permute-start(bf16[128,4608]{1,0:T(8,128)(2,1)} %refs_4_.5), channel_id=1, source_target_pairs={{0,4},{4,0},{8,12},{12,8},{1,5},{5,1},{9,13},{13,9},{2,6},{6,2},{1... | collective-permute-start | bytes 3538952 | tf_op jit(solution)/shard_map/ppermute | solution.py:480
  3.7 27.9 %collective-permute-start.5 = (bf16[128,4608]{1,0:T(8,128)(2,1)}, bf16[128,4608]{1,0:T(8,128)(2,1)S(1)}, u32[]{:S(2)}, u32[]{:S(2)}) collective-permute-start(bf16[128,4608]{1,0:T(8,128)(2,1)} %refs_4_.5), channel_id=1, source_target_pairs={{4,8},{8,4},{5,9},{9,5},{6,10},{10,6},{7,11},{11,7},{20,24},{24,20... | collective-permute-start | bytes 3538952 | tf_op jit(solution)/shard_map/ppermute | solution.py:481
  4.5 25.5 %collective-permute-start.1 = (bf16[128,1536]{1,0:T(8,128)(2,1)}, bf16[128,1536]{1,0:T(8,128)(2,1)}, u32[]{:S(2)}, u32[]{:S(2)}) collective-permute-start(bf16[128,1536]{1,0:T(8,128)(2,1)} %param.5), channel_id=1, source_target_pairs={{0,2},{1,3},{2,0},{3,1},{4,6},{5,7},{6,4},{7,5},{8,10},{9,11},{10,... | collective-permute-start | bytes 1179656 | tf_op jit(solution)/shard_map/ppermute | solution.py:486
  6.0 24.0 %collective-permute-start = (bf16[128,1536]{1,0:T(8,128)(2,1)}, bf16[128,1536]{1,0:T(8,128)(2,1)S(1)}, u32[]{:S(2)}, u32[]{:S(2)}) collective-permute-start(bf16[128,1536]{1,0:T(8,128)(2,1)} %param.5), channel_id=1, source_target_pairs={{0,1},{1,0},{2,3},{3,2},{4,5},{5,4},{6,7},{7,6},{8,9},{9,8},{10,11... | collective-permute-start | bytes 1179656 | tf_op jit(solution)/shard_map/ppermute | solution.py:485
  29.9 3.2 %copy-start.1 = (bf16[128,4608]{1,0:T(8,128)(2,1)}, bf16[128,4608]{1,0:T(8,128)(2,1)S(1)}, u32[]{:S(2)}) copy-start(bf16[128,4608]{1,0:T(8,128)(2,1)S(1)} %collective-permute-done.2.refs_5_) | copy-start | bytes 3538948
  29.9 21.0 %copy-start.7 = (bf16[128,1536]{1,0:T(8,128)(2,1)S(1)}, bf16[128,1536]{1,0:T(8,128)(2,1)}, u32[]{:S(2)}) copy-start(bf16[128,1536]{1,0:T(8,128)(2,1)} %param.5) | copy-start | bytes 1179652
  30.0 3.0 %copy-start.8 = (bf16[128,1536]{1,0:T(8,128)(2,1)}, bf16[128,1536]{1,0:T(8,128)(2,1)S(1)}, u32[]{:S(2)}) copy-start(bf16[128,1536]{1,0:T(8,128)(2,1)S(1)} %collective-permute-done) | copy-start | bytes 1179652
  30.0 3.0 %collective-permute-start.3 = (bf16[128,2304]{1,0:T(8,128)(2,1)S(1)}, bf16[128,2304]{1,0:T(8,128)(2,1)}, u32[]{:S(2)}, u32[]{:S(2)}) collective-permute-start(bf16[128,2304]{1,0:T(8,128)(2,1)S(1)} %slice.24), channel_id=1, source_target_pairs={{4,8},{8,4},{5,9},{9,5},{6,10},{10,6},{7,11},{11,7},{20,24},{24,20... | collective-permute-start | bytes 1769480 | tf_op jit(solution)/shard_map/ppermute | solution.py:487
  31.6 2.3 copy-start.2
  31.7 17.3 %collective-permute-start.7 = (bf16[128,2304]{1,0:T(8,128)(2,1)S(1)}, bf16[128,2304]{1,0:T(8,128)(2,1)}, u32[]{:S(2)}, u32[]{:S(2)}) collective-permute-start(bf16[128,2304]{1,0:T(8,128)(2,1)S(1)} %slice.27), channel_id=1, source_target_pairs={{4,0},{8,12},{5,1},{9,13},{6,2},{10,14},{7,3},{11,15},{20,16},{24,... | collective-permute-start | bytes 1769480 | tf_op jit(solution)/shard_map/ppermute | solution.py:497
  33.0 18.0 %collective-permute-start.4 = (bf16[128,1536]{1,0:T(8,128)(2,1)}, bf16[128,1536]{1,0:T(8,128)(2,1)}, u32[]{:S(2)}, u32[]{:S(2)}) collective-permute-start(bf16[128,1536]{1,0:T(8,128)(2,1)} %collective-permute-done.1), channel_id=1, source_target_pairs={{0,1},{1,0},{2,3},{3,2},{4,5},{5,4},{6,7},{7,6},{8,9},{9,8},{10,11... | collective-permute-start | bytes 1179656 | tf_op jit(solution)/shard_map/ppermute | solution.py:489
  33.1 17.9 %copy-start.9 = (bf16[128,1536]{1,0:T(8,128)(2,1)S(1)}, bf16[128,1536]{1,0:T(8,128)(2,1)}, u32[]{:S(2)}) copy-start(bf16[128,1536]{1,0:T(8,128)(2,1)} %copy-done.8) | copy-start | bytes 1179652
  33.9 21.8 %collective-permute-start.6 = (bf16[128,768]{1,0:T(8,128)(2,1)S(1)}, bf16[128,768]{1,0:T(8,128)(2,1)S(1)}, u32[]{:S(2)}, u32[]{:S(2)}) collective-permute-start(bf16[128,768]{1,0:T(8,128)(2,1)S(1)} %slice.26), channel_id=1, source_target_pairs={{4,8},{8,4},{5,9},{9,5},{6,10},{10,6},{7,11},{11,7},{20,24},{24,20... | collective-permute-start | bytes 589832 | tf_op jit(solution)/shard_map/ppermute | solution.py:488
  49.0 18.6 %collective-permute-start.8 = (bf16[128,2304]{1,0:T(8,128)(2,1)}, bf16[128,2304]{1,0:T(8,128)(2,1)S(1)}, u32[]{:S(2)}, u32[]{:S(2)}) collective-permute-start(bf16[128,2304]{1,0:T(8,128)(2,1)} %collective-permute-done.3.refs_8_), channel_id=1, source_target_pairs={{4,0},{8,12},{5,1},{9,13},{6,2},{10,14},{7,3},{11,15},{20,16},{24,... | collective-permute-start | bytes 1769480 | tf_op jit(solution)/shard_map/ppermute | solution.py:498
  50.3 3.3 %collective-permute-start.10 = (bf16[128,1536]{1,0:T(8,128)(2,1)}, bf16[128,1536]{1,0:T(8,128)(2,1)S(1)}, u32[]{:S(2)}, u32[]{:S(2)}) collective-permute-start(bf16[128,1536]{1,0:T(8,128)(2,1)} %slice.29), channel_id=1, source_target_pairs={{4,8},{8,4},{5,9},{9,5},{6,10},{10,6},{7,11},{11,7},{20,24},{24,20... | collective-permute-start | bytes 1179656 | tf_op jit(solution)/shard_map/ppermute | solution.py:488
  53.3 1.0 slice-start.1
  53.4 2.4 slice-start
  54.3 26.3 %copy-start.5 = (bf16[128,1536]{1,0:T(8,128)(2,1)}, bf16[128,1536]{1,0:T(8,128)(2,1)S(1)}, u32[]{:S(2)}) copy-start(bf16[128,1536]{1,0:T(8,128)(2,1)S(1)} %collective-permute-done.10.refs_8_) | copy-start | bytes 1179652
  54.4 31.6 %collective-permute-start.11 = (bf16[256,1536]{1,0:T(8,128)(2,1)S(1)}, bf16[256,1536]{1,0:T(8,128)(2,1)S(1)}, u32[]{:S(2)}, u32[]{:S(2)}) collective-permute-start(bf16[256,1536]{1,0:T(8,128)(2,1)S(1)} %pad_maximum_fusion.1), channel_id=1, source_target_pairs={{4,0},{8,12},{5,1},{9,13},{6,2},{10,14},{7,3},{11,15},{20,16},{24,... | collective-permute-start | bytes 2359304 | tf_op jit(solution)/shard_map/ppermute | solution.py:503
  55.7 24.9 %copy-start.6 = (bf16[128,768]{1,0:T(8,128)(2,1)}, bf16[128,768]{1,0:T(8,128)(2,1)S(1)}, u32[]{:S(2)}) copy-start(bf16[128,768]{1,0:T(8,128)(2,1)S(1)} %collective-permute-done.6.refs_8_) | copy-start | bytes 589828
  67.6 0.8 copy-start.10
  80.6 16.4 %collective-permute-start.9 = (bf16[256,768]{1,0:T(8,128)(2,1)S(1)}, bf16[256,768]{1,0:T(8,128)(2,1)S(1)}, u32[]{:S(2)}, u32[]{:S(2)}) collective-permute-start(bf16[256,768]{1,0:T(8,128)(2,1)S(1)} %pad_maximum_fusion.2), channel_id=1, source_target_pairs={{4,0},{8,12},{5,1},{9,13},{6,2},{10,14},{7,3},{11,15},{20,16},{24,... | collective-permute-start | bytes 1179656 | tf_op jit(solution)/shard_map/ppermute | solution.py:503
  86.0 0.9 copy-start.3
  97.1 0.7 copy-start.4
  103.9 2.4 collective-permute-start.12
  106.4 11.2 %collective-permute-start.13 = (bf16[768,256]{1,0:T(8,128)(2,1)S(1)}, bf16[768,256]{1,0:T(8,128)(2,1)S(1)}, u32[]{:S(2)}, u32[]{:S(2)}) collective-permute-start(bf16[768,256]{1,0:T(8,128)(2,1)S(1)} %add_convert_fusion.8), channel_id=1, source_target_pairs={{0,2},{1,3},{2,0},{3,1},{4,6},{5,7},{6,4},{7,5},{8,10},{9,11},{10,... | collective-permute-start | bytes 1179656 | tf_op jit(solution)/shard_map/ppermute | solution.py:427
  117.7 2.4 collective-permute-start.14
  120.0 20.3 %copy-start = (bf16[1536,256]{1,0:T(8,128)(2,1)S(1)}, bf16[1536,256]{1,0:T(8,128)(2,1)}, u32[]{:S(2)}) copy-start(bf16[1536,256]{1,0:T(8,128)(2,1)} %refs_0_.2) | copy-start | bytes 2359300
  127.9 3.3 %collective-permute-start.16 = (f32[2,8,128]{2,1,0:T(8,128)S(1)}, f32[2,8,128]{2,1,0:T(8,128)S(1)}, u32[]{:S(2)}, u32[]{:S(2)}) collective-permute-start(f32[2,8,128]{2,1,0:T(8,128)S(1)} %get-tuple-element.58), channel_id=1, source_target_pairs={{0,1},{1,2},{2,3},{3,0},{4,5},{5,6},{6,7},{7,4},{8,9},{9,10},{10,1... | collective-permute-start | bytes 24584 | tf_op jit(solution)/shard_map/ppermute | solution.py:393
  128.1 3.1 %collective-permute-start.17 = (f32[2,8,128]{2,1,0:T(8,128)S(1)}, f32[2,8,128]{2,1,0:T(8,128)S(1)}, u32[]{:S(2)}, u32[]{:S(2)}) collective-permute-start(f32[2,8,128]{2,1,0:T(8,128)S(1)} %get-tuple-element.58), channel_id=1, source_target_pairs={{0,3},{1,0},{2,1},{3,2},{4,7},{5,4},{6,5},{7,6},{8,11},{9,8},{10,9... | collective-permute-start | bytes 24584 | tf_op jit(solution)/shard_map/ppermute | solution.py:393
  129.7 3.7 %collective-permute-start.15 = (f32[2,8,128]{2,1,0:T(8,128)S(1)}, f32[2,8,128]{2,1,0:T(8,128)S(1)}, u32[]{:S(2)}, u32[]{:S(2)}) collective-permute-start(f32[2,8,128]{2,1,0:T(8,128)S(1)} %get-tuple-element.58), channel_id=1, source_target_pairs={{0,2},{1,3},{2,0},{3,1},{4,6},{5,7},{6,4},{7,5},{8,10},{9,11},{10,... | collective-permute-start | bytes 24584 | tf_op jit(solution)/shard_map/ppermute | solution.py:393
  133.4 5.4 %collective-permute-start.18 = (f32[2,8,128]{2,1,0:T(8,128)S(1)}, f32[2,8,128]{2,1,0:T(8,128)S(1)}, u32[]{:S(2)}, u32[]{:S(2)}) collective-permute-start(f32[2,8,128]{2,1,0:T(8,128)S(1)} %add_add_fusion.1.refs_2_), channel_id=1, source_target_pairs={{0,4},{4,8},{8,12},{12,0},{1,5},{5,9},{9,13},{13,1},{2,6},{6,10},{... | collective-permute-start | bytes 24584 | tf_op jit(solution)/shard_map/ppermute | solution.py:393
  133.4 5.4 %collective-permute-start.19 = (f32[2,8,128]{2,1,0:T(8,128)S(1)}, f32[2,8,128]{2,1,0:T(8,128)S(1)}, u32[]{:S(2)}, u32[]{:S(2)}) collective-permute-start(f32[2,8,128]{2,1,0:T(8,128)S(1)} %add_add_fusion.1.refs_2_), channel_id=1, source_target_pairs={{0,8},{4,12},{8,0},{12,4},{1,9},{5,13},{9,1},{13,5},{2,10},{6,14},... | collective-permute-start | bytes 24584 | tf_op jit(solution)/shard_map/ppermute | solution.py:393
  136.7 3.7 %collective-permute-start.20 = (f32[2,8,128]{2,1,0:T(8,128)S(1)}, f32[2,8,128]{2,1,0:T(8,128)S(1)}, u32[]{:S(2)}, u32[]{:S(2)}) collective-permute-start(f32[2,8,128]{2,1,0:T(8,128)S(1)} %add_add_fusion.1.refs_2_), channel_id=1, source_target_pairs={{0,12},{4,0},{8,4},{12,8},{1,13},{5,1},{9,5},{13,9},{2,14},{6,2},{... | collective-permute-start | bytes 24584 | tf_op jit(solution)/shard_map/ppermute | solution.py:393
  148.2 19.3 %collective-permute-start.21 = (bf16[256,1152]{1,0:T(8,128)(2,1)}, bf16[256,1152]{1,0:T(8,128)(2,1)}, u32[]{:S(2)}, u32[]{:S(2)}) collective-permute-start(bf16[256,1152]{1,0:T(8,128)(2,1)} %partial_pass.4.k_ref), channel_id=1, source_target_pairs={{0,4},{12,8},{1,5},{13,9},{2,6},{14,10},{3,7},{15,11},{16,20},{28,... | collective-permute-start | bytes 1769480 | tf_op jit(solution)/shard_map/ppermute | solution.py:450
  158.5 21.3 %collective-permute-start.22 = (bf16[256,1152]{1,0:T(8,128)(2,1)S(1)}, bf16[256,1152]{1,0:T(8,128)(2,1)S(1)}, u32[]{:S(2)}, u32[]{:S(2)}) collective-permute-start(bf16[256,1152]{1,0:T(8,128)(2,1)S(1)} %partial_pass.5.k_ref), channel_id=1, source_target_pairs={{0,4},{12,8},{1,5},{13,9},{2,6},{14,10},{3,7},{15,11},{16,20},{28,... | collective-permute-start | bytes 1769480 | tf_op jit(solution)/shard_map/ppermute | solution.py:450
  166.2 24.3 %collective-permute-start.24 = (bf16[256,1152]{1,0:T(8,128)(2,1)S(1)}, bf16[256,1152]{1,0:T(8,128)(2,1)S(1)}, u32[]{:S(2)}, u32[]{:S(2)}) collective-permute-start(bf16[256,1152]{1,0:T(8,128)(2,1)S(1)} %partial_pass.6), channel_id=1, source_target_pairs={{0,4},{12,8},{1,5},{13,9},{2,6},{14,10},{3,7},{15,11},{16,20},{28,... | collective-permute-start | bytes 1769480 | tf_op jit(solution)/shard_map/ppermute | solution.py:450
  168.9 11.7 %collective-permute-start.23 = (bf16[256,1152]{1,0:T(8,128)(2,1)S(1)}, bf16[256,1152]{1,0:T(8,128)(2,1)S(1)}, u32[]{:S(2)}, u32[]{:S(2)}) collective-permute-start(bf16[256,1152]{1,0:T(8,128)(2,1)S(1)} %add_convert_fusion.7.k_ref), channel_id=1, source_target_pairs={{4,8},{8,4},{5,9},{9,5},{6,10},{10,6},{7,11},{11,7},{20,24},{24,20... | collective-permute-start | bytes 1769480 | tf_op jit(solution)/shard_map/ppermute | solution.py:456
  176.1 24.0 %collective-permute-start.26 = (bf16[256,1152]{1,0:T(8,128)(2,1)S(1)}, bf16[256,1152]{1,0:T(8,128)(2,1)S(1)}, u32[]{:S(2)}, u32[]{:S(2)}) collective-permute-start(bf16[256,1152]{1,0:T(8,128)(2,1)S(1)} %partial_pass.7), channel_id=1, source_target_pairs={{0,4},{12,8},{1,5},{13,9},{2,6},{14,10},{3,7},{15,11},{16,20},{28,... | collective-permute-start | bytes 1769480 | tf_op jit(solution)/shard_map/ppermute | solution.py:450
  179.9 11.4 %collective-permute-start.25 = (bf16[256,1152]{1,0:T(8,128)(2,1)S(1)}, bf16[256,1152]{1,0:T(8,128)(2,1)S(1)}, u32[]{:S(2)}, u32[]{:S(2)}) collective-permute-start(bf16[256,1152]{1,0:T(8,128)(2,1)S(1)} %add_convert_fusion.6), channel_id=1, source_target_pairs={{4,8},{8,4},{5,9},{9,5},{6,10},{10,6},{7,11},{11,7},{20,24},{24,20... | collective-permute-start | bytes 1769480 | tf_op jit(solution)/shard_map/ppermute | solution.py:456
  180.8 20.1 %collective-permute-start.27 = (bf16[256,1152]{1,0:T(8,128)(2,1)S(1)}, bf16[256,1152]{1,0:T(8,128)(2,1)S(1)}, u32[]{:S(2)}, u32[]{:S(2)}) collective-permute-start(bf16[256,1152]{1,0:T(8,128)(2,1)S(1)} %add_convert_fusion.5.t_ref), channel_id=1, source_target_pairs={{4,0},{8,12},{5,1},{9,13},{6,2},{10,14},{7,3},{11,15},{20,16},{24,... | collective-permute-start | bytes 1769480 | tf_op jit(solution)/shard_map/ppermute | solution.py:462
  190.6 13.6 %collective-permute-start.28 = (bf16[256,1152]{1,0:T(8,128)(2,1)S(1)}, bf16[256,1152]{1,0:T(8,128)(2,1)S(1)}, u32[]{:S(2)}, u32[]{:S(2)}) collective-permute-start(bf16[256,1152]{1,0:T(8,128)(2,1)S(1)} %add_convert_fusion.4), channel_id=1, source_target_pairs={{4,8},{8,4},{5,9},{9,5},{6,10},{10,6},{7,11},{11,7},{20,24},{24,20... | collective-permute-start | bytes 1769480 | tf_op jit(solution)/shard_map/ppermute | solution.py:456
  191.5 17.0 %collective-permute-start.29 = (bf16[256,1152]{1,0:T(8,128)(2,1)S(1)}, bf16[256,1152]{1,0:T(8,128)(2,1)S(1)}, u32[]{:S(2)}, u32[]{:S(2)}) collective-permute-start(bf16[256,1152]{1,0:T(8,128)(2,1)S(1)} %add_convert_fusion.3.t_ref), channel_id=1, source_target_pairs={{4,0},{8,12},{5,1},{9,13},{6,2},{10,14},{7,3},{11,15},{20,16},{24,... | collective-permute-start | bytes 1769480 | tf_op jit(solution)/shard_map/ppermute | solution.py:462
  200.2 11.6 %collective-permute-start.30 = (bf16[256,1152]{1,0:T(8,128)(2,1)S(1)}, bf16[256,1152]{1,0:T(8,128)(2,1)S(1)}, u32[]{:S(2)}, u32[]{:S(2)}) collective-permute-start(bf16[256,1152]{1,0:T(8,128)(2,1)S(1)} %add_convert_fusion.2), channel_id=1, source_target_pairs={{4,8},{8,4},{5,9},{9,5},{6,10},{10,6},{7,11},{11,7},{20,24},{24,20... | collective-permute-start | bytes 1769480 | tf_op jit(solution)/shard_map/ppermute | solution.py:456
  204.4 16.8 %collective-permute-start.31 = (bf16[256,1152]{1,0:T(8,128)(2,1)S(1)}, bf16[256,1152]{1,0:T(8,128)(2,1)S(1)}, u32[]{:S(2)}, u32[]{:S(2)}) collective-permute-start(bf16[256,1152]{1,0:T(8,128)(2,1)S(1)} %add_convert_fusion.1.t_ref), channel_id=1, source_target_pairs={{4,0},{8,12},{5,1},{9,13},{6,2},{10,14},{7,3},{11,15},{20,16},{24,... | collective-permute-start | bytes 1769480 | tf_op jit(solution)/shard_map/ppermute | solution.py:462
  212.0 21.2 %collective-permute-start.32 = (bf16[256,1152]{1,0:T(8,128)(2,1)S(1)}, bf16[256,1152]{1,0:T(8,128)(2,1)S(1)}, u32[]{:S(2)}, u32[]{:S(2)}) collective-permute-start(bf16[256,1152]{1,0:T(8,128)(2,1)S(1)} %add_convert_fusion.t_ref), channel_id=1, source_target_pairs={{4,0},{8,12},{5,1},{9,13},{6,2},{10,14},{7,3},{11,15},{20,16},{24,... | collective-permute-start | bytes 1769480 | tf_op jit(solution)/shard_map/ppermute | solution.py:462
  236.6 3.2 %collective-permute-start.34 = (f32[2,8,128]{2,1,0:T(8,128)S(1)}, f32[2,8,128]{2,1,0:T(8,128)S(1)}, u32[]{:S(2)}, u32[]{:S(2)}) collective-permute-start(f32[2,8,128]{2,1,0:T(8,128)S(1)} %get-tuple-element.82), channel_id=1, source_target_pairs={{0,1},{1,2},{2,3},{3,0},{4,5},{5,6},{6,7},{7,4},{8,9},{9,10},{10,1... | collective-permute-start | bytes 24584 | tf_op jit(solution)/shard_map/ppermute | solution.py:393
  236.6 3.1 %collective-permute-start.35 = (f32[2,8,128]{2,1,0:T(8,128)S(1)}, f32[2,8,128]{2,1,0:T(8,128)S(1)}, u32[]{:S(2)}, u32[]{:S(2)}) collective-permute-start(f32[2,8,128]{2,1,0:T(8,128)S(1)} %get-tuple-element.82), channel_id=1, source_target_pairs={{0,3},{1,0},{2,1},{3,2},{4,7},{5,4},{6,5},{7,6},{8,11},{9,8},{10,9... | collective-permute-start | bytes 24584 | tf_op jit(solution)/shard_map/ppermute | solution.py:393
  238.4 3.7 %collective-permute-start.33 = (f32[2,8,128]{2,1,0:T(8,128)S(1)}, f32[2,8,128]{2,1,0:T(8,128)S(1)}, u32[]{:S(2)}, u32[]{:S(2)}) collective-permute-start(f32[2,8,128]{2,1,0:T(8,128)S(1)} %get-tuple-element.82), channel_id=1, source_target_pairs={{0,2},{1,3},{2,0},{3,1},{4,6},{5,7},{6,4},{7,5},{8,10},{9,11},{10,... | collective-permute-start | bytes 24584 | tf_op jit(solution)/shard_map/ppermute | solution.py:393
  242.0 5.5 %collective-permute-start.36 = (f32[2,8,128]{2,1,0:T(8,128)S(1)}, f32[2,8,128]{2,1,0:T(8,128)S(1)}, u32[]{:S(2)}, u32[]{:S(2)}) collective-permute-start(f32[2,8,128]{2,1,0:T(8,128)S(1)} %add_add_fusion.refs_8_), channel_id=1, source_target_pairs={{0,4},{4,8},{8,12},{12,0},{1,5},{5,9},{9,13},{13,1},{2,6},{6,10},{... | collective-permute-start | bytes 24584 | tf_op jit(solution)/shard_map/ppermute | solution.py:393
  242.0 5.5 %collective-permute-start.37 = (f32[2,8,128]{2,1,0:T(8,128)S(1)}, f32[2,8,128]{2,1,0:T(8,128)S(1)}, u32[]{:S(2)}, u32[]{:S(2)}) collective-permute-start(f32[2,8,128]{2,1,0:T(8,128)S(1)} %add_add_fusion.refs_8_), channel_id=1, source_target_pairs={{0,8},{4,12},{8,0},{12,4},{1,9},{5,13},{9,1},{13,5},{2,10},{6,14},... | collective-permute-start | bytes 24584 | tf_op jit(solution)/shard_map/ppermute | solution.py:393
  244.5 3.7 %collective-permute-start.38 = (f32[2,8,128]{2,1,0:T(8,128)S(1)}, f32[2,8,128]{2,1,0:T(8,128)S(1)}, u32[]{:S(2)}, u32[]{:S(2)}) collective-permute-start(f32[2,8,128]{2,1,0:T(8,128)S(1)} %add_add_fusion.refs_8_), channel_id=1, source_target_pairs={{0,12},{4,0},{8,4},{12,8},{1,13},{5,1},{9,5},{13,9},{2,14},{6,2},{... | collective-permute-start | bytes 24584 | tf_op jit(solution)/shard_map/ppermute | solution.py:393
